TPU v7x, 256 devices: a whole 4x4x8 slice. The times are simulated.
256 devices in a mesh: dp: 64 (over x, z, core), proto: 4 (over y).
Axes of the slice: x: 4, y: 4, z: 8, core: 2. Of those that a mesh axis runs over, the one named last changes fastest.
Arguments:
- embeddings: bfloat16 [32768, 256], P('dp'), may hold values from -1.5 to 1.5
- prototypes: bfloat16 [16384, 256], P('proto'), may hold values from -0.35 to 0.35
- pair_index: int32 [32768], P('dp'), may hold values from 0 to 511, as said below
Outputs:
- grad_embeddings: float32 [32768, 256], P('dp')
- grad_prototypes: float32 [16384, 256], P(('proto', 'dp'))
Inputs may be any that keep to these rules, and one draw needn't show every extreme that they name: Within each aligned block of 512 rows the rows are paired off: pair_index maps each row to its partner, partner of partner is the row itself, and no row is its own partner.
All inputs are finite; a program needn't handle non-finite values.
Results may differ from a plain program's by a relative error of at most 0.0033.
Values may be sent and summed in bfloat16 or wider, within the bound.
A program may use at most 128 MiB of HBM per device.

v0:
```python
import jax
import jax.numpy as jnp
from jax import lax
from jax.sharding import PartitionSpec as P

ITERS = 3


sink_eps = 0.05
sharpness_divisor = 0.1
objective_factor = 1.0


def unit_rows(matrix):
    values = matrix.astype(jnp.float32)
    norms = jnp.sqrt(jnp.sum(values * values, axis=1, keepdims=True) + 1e-06)
    return (values / norms, norms)


def column_sum(kernel, row_scale):
    local = jnp.dot(row_scale, kernel, precision=lax.Precision.HIGHEST)
    return lax.psum(local, "dp")


def row_sum(local):
    return lax.psum(local, "proto")


def body(embeddings, prototypes, pair_index):
    hp = lax.Precision.HIGHEST
    unit_z, norm_z = unit_rows(embeddings)
    unit_c, norm_c = unit_rows(prototypes)
    z_hat = unit_z.astype(jnp.bfloat16)
    c_hat = unit_c.astype(jnp.bfloat16)
    cluster_affinity = lax.dot_general(
        z_hat, c_hat, (((1,), (1,)), ((), ())), preferred_element_type=jnp.float32
    )
    kernel = jnp.exp(cluster_affinity / sink_eps)
    raised_power = jnp.exp(cluster_affinity / sharpness_divisor)
    exp_local = jnp.sum(raised_power, axis=1)
    row_scale = jnp.ones((cluster_affinity.shape[0],), jnp.float32)
    for step in range(ITERS):
        col_scale = 1.0 / column_sum(kernel, row_scale)
        row_scale = 1.0 / row_sum(jnp.dot(kernel, col_scale, precision=hp))
    exp_total = lax.psum(exp_local, "proto")
    predicted_likelihood = raised_power / exp_total[:, None]
    codes = kernel * col_scale[None, :] * row_scale[:, None]
    crossed_assignment = jnp.take(codes, pair_index, axis=0)
    affinity_derivative = (
        objective_factor / sharpness_divisor * (predicted_likelihood - crossed_assignment)
    ).astype(jnp.bfloat16)
    grad_local = jnp.dot(affinity_derivative, c_hat, preferred_element_type=jnp.float32)
    grad_zhat = lax.psum(grad_local, "proto")
    grad_embeddings = (
        grad_zhat - unit_z * jnp.sum(unit_z * grad_zhat, axis=1, keepdims=True)
    ) / norm_z
    owned = prototypes.shape[0] // lax.axis_size("dp")
    grad_chat = lax.psum_scatter(
        lax.dot_general(
            affinity_derivative, z_hat, (((0,), (0,)), ((), ())), preferred_element_type=jnp.float32
        ),
        "dp",
        scatter_dimension=0,
        tiled=True,
    )
    offset = lax.axis_index("dp") * owned
    own_unit = lax.dynamic_slice_in_dim(unit_c, offset, owned, 0)
    own_norm = lax.dynamic_slice_in_dim(norm_c, offset, owned, 0)
    grad_prototypes = (
        grad_chat - own_unit * jnp.sum(own_unit * grad_chat, axis=1, keepdims=True)
    ) / own_norm
    return (grad_embeddings, grad_prototypes)


def solution(mesh):
    in_specs = (P("dp", None), P("proto", None), P("dp"))
    out_specs = (P("dp", None), P(("proto", "dp"), None))
    return jax.shard_map(body, mesh=mesh, in_specs=in_specs, out_specs=out_specs, check_vma=False)
```

profile of v0, /device:TPU:1, one launch (start us, length us, event | category | flops | bytes accessed | tf_op | source)
XLA Modules:
  0.0 1022.6 jit_solution(11469025001034059647)
XLA Ops:
  8.0 0.7 compare_select_fusion
  8.7 0.7 compare_and_fusion
  9.4 2.2 fusion.1
  11.6 1.1 fusion.12
  12.8 3.8 fusion
  16.5 3.2 copy-done
  19.8 4.7 fusion.7
  24.5 249.4 %psum.57 = f32[4096]{0:T(1024)S(1)} all-reduce(f32[4096]{0:T(1024)S(1)} %bitcast.23), channel_id=1, replica_groups=mesh['dp'=64,'proto'=4] {'dp'}, use_global_device_ids=true, to_apply=%region_4.0 | all-reduce | flops 4096 | bytes 32768 | tf_op jit(solution)/shard_map/psum | solution.py:22
  273.9 10.2 fusion.6
  284.1 8.9 psum.58
  293.0 7.1 fusion.5
  300.1 248.2 %psum.59 = f32[4096]{0:T(1024)S(1)} all-reduce(f32[4096]{0:T(1024)S(1)} %bitcast.20), channel_id=1, replica_groups=mesh['dp'=64,'proto'=4] {'dp'}, use_global_device_ids=true, to_apply=%region_6.0 | all-reduce | flops 4096 | bytes 32768 | tf_op jit(solution)/shard_map/psum | solution.py:22
  548.3 10.2 fusion.4
  558.4 6.0 psum.60
  564.4 7.1 fusion.3
  571.5 248.1 %psum.61 = f32[4096]{0:T(1024)S(1)} all-reduce(f32[4096]{0:T(1024)S(1)} %bitcast.22), channel_id=1, replica_groups=mesh['dp'=64,'proto'=4] {'dp'}, use_global_device_ids=true, to_apply=%region_8.0 | all-reduce | flops 4096 | bytes 32768 | tf_op jit(solution)/shard_map/psum | solution.py:22
  819.6 10.2 fusion.2
  829.8 7.7 all-reduce
  837.5 8.4 multiply_multiply_fusion
  846.0 12.2 %gather_fusion = f32[512,4096]{1,0:T(8,128)} fusion(f32[512,4096]{1,0:T(8,128)} %multiply_multiply_fusion, s32[1024]{0:T(1024)S(1)} %pad_clamp_fusion), kind=kCustom, calls=%fused_computation | custom fusion | bytes 16779264 | tf_op jit(solution)/shard_map/jit(_take)/gather | solution.py:48
  858.2 7.3 multiply_convert_fusion
  865.5 2.0 copy-done.2
  867.4 2.2 fusion.8
  869.8 5.5 fusion.13
  875.3 0.1 dynamic-slice.3
  875.4 2.3 convert_divide_fusion
  877.7 37.0 %all-reduce.3.cloned.1.call-done = f32[512,256]{1,0:T(8,128)} async-done(((f32[512,256]{1,0:T(8,128)}), f32[512,256]{1,0:T(8,128)}) %all-reduce.3.cloned.1.call-update) | async-done | bytes 524304 | tf_op jit(solution)/shard_map/psum | solution.py:53
  914.7 1.3 multiply_reduce_fusion
  916.0 2.1 subtract_divide_fusion
  918.1 94.5 %reduce-scatter.2.cloned.1.call-done = f32[64,256]{1,0:T(8,128)} async-done(((f32[4096,256]{1,0:T(8,128)}), f32[64,256]{1,0:T(8,128)}) %reduce-scatter.2.cloned.1.call-update) | async-done | bytes 65552 | tf_op jit(solution)/shard_map/reduce_scatter | solution.py:58
  1012.6 1.0 multiply_reduce_fusion.1
  1013.6 1.6 subtract_divide_fusion.1
  (19 shorter events, 0.2 us)
Async XLA Ops:
  8.0 906.7 %all-reduce.3.cloned.1.call-start = ((), (), s32[]{:S(2)}) async-start(), calls=%async_computation.1 | async-start | bytes 1048576 | tf_op jit(solution)/shard_map/psum | solution.py:53
  16.5 3.2 copy-start
  858.2 9.3 copy-start.1
  865.5 2.0 copy-start.2
  867.4 2.3 copy-start.3
  869.7 142.9 %reduce-scatter.2.cloned.1.call-start = ((), (), s32[]{:S(2)}) async-start(), calls=%async_computation.2 | async-start | bytes 4259840 | tf_op jit(solution)/shard_map/reduce_scatter | solution.py:58
Sparse Core Ops, SparseCore 0:
  869.8 44.8 all-reduce.2
Sparse Core Ops, SparseCore 1:
  875.4 137.2 reduce-scatter.1
where the time goes:
time: 1030 us; the launch traced here: 1020 us
  blocking collectives  768 us (75%)
  waiting for transfers between devices  132 us (13%)
  matrix products  60.9 us (6%)
  other arithmetic  28.7 us (3%)
  local copies, waits for them, and re-layouts  17.5 us (2%)
  between operations  15.6 us (2%)
    psum x3, blocking collectives, column_sum(): return lax.psum(local, 'dp')  746 us
    reduce_scatter x1, waiting for transfers between devices, body(): lax.psum_scatter(lax.dot_general(affinity_derivative, z_hat, (((0,), (0,)...  94.5 us
    psum x1, waiting for transfers between devices, body(): grad_zhat = lax.psum(grad_local, 'proto')  37 us
    dot_general x3, matrix products, body(): row_scale = 1.0 / row_sum(jnp.dot(kernel, col_scale, precision=hp))  30.5 us
    psum x3, blocking collectives, row_sum(): return lax.psum(local, 'proto')  22.6 us
  transfers between devices with their start and end apart: 2, of which 2 were waited for; matrix products, arithmetic and copies ran while one was open for 1% of the time, Pallas kernels for 0%

commit v1 on v0

v1 whole, which is shorter than its diff:
```python
import jax
import jax.numpy as jnp
from jax import lax
from jax.experimental import pallas as pl
from jax.experimental.pallas import tpu as pltpu
from jax.sharding import PartitionSpec as P

X, Z, C, Y = 4, 8, 2, 4
MESH = pl.DeviceIdType.MESH
F32, BF16 = jnp.float32, jnp.bfloat16
NT = (((1,), (1,)), ((), ()))
NN = (((1,), (0,)), ((), ()))


def ring(k, n):
    return min(k, n - k)


def offsets(axes):
    span = [n if a in axes else 1 for a, n in zip("xzcy", (X, Z, C, Y))]
    out = [
        (a, b, e, f)
        for a in range(span[0])
        for b in range(span[1])
        for e in range(span[2])
        for f in range(span[3])
        if a or b or e or f
    ]
    out.sort(key=lambda t: -(4 * (ring(t[0], X) + ring(t[1], Z) + ring(t[3], Y)) + t[2]))
    return out


def dot(a, b, dims=NN):
    return lax.dot_general(a, b, dims, preferred_element_type=F32)


def unit(values):
    norm = jnp.sqrt(jnp.sum(values * values, axis=1, keepdims=True) + 1e-06)
    return values / norm, norm


def spread(row):
    return jnp.broadcast_to(row, (128, 128)).T


def make_kernel(B, D, NC):
    RT, RC, CC, TC = C * B, C * B // 128, NC // 128, NC // X
    OB = TC // Z
    BC = B // 128
    HB = B // 2
    XZ, YC, XYC = offsets("xz"), offsets("yc"), offsets("xyc")

    def kernel(
        emb_ref, proto_ref, pair_ref, gz_ref, gc_ref,
        praw, chat, ep, perm, permt, zall, E, K, ET, WT, G, GT, colacc, racc, rb, rpb, c3b,
        crow, rrow, rp4, r34, csend, crecv, rsend1, rrecv1, rsend2, rrecv2, rsend3, rrecv3,
        gpart, ksend, krecv, tpart, zsend, zrecv, ysend, yrecv, yall,
        lsem, core_s, core_r, xs, xr, fs, fr, cs, cr, rs, rr, ps, pr, ks, kr, zs, zr, ys, yr, gs, gr,
    ):
        dp = lax.axis_index("dp")
        iy = lax.axis_index("proto")
        ix, iz, ic = dp // (Z * C), (dp // C) % Z, dp % C

        def dev(o):
            a, b, e, f = o
            nx = (ix + a) % X if a else ix
            nz = (iz + b) % Z if b else iz
            nc = (ic + e) % C if e else ic
            ny = (iy + f) % Y if f else iy
            return {"dp": (nx * Z + nz) * C + nc, "proto": ny}

        def send(src, dst, s, r, o):
            pltpu.make_async_remote_copy(
                src_ref=src, dst_ref=dst, send_sem=s, recv_sem=r, device_id=dev(o), device_id_type=MESH
            ).start()

        def take(ref, sem):
            pltpu.make_async_copy(ref, ref, sem).wait()

        load = pltpu.make_async_copy(proto_ref.at[:, ic], praw, lsem.at[0])
        load.start()
        barrier = pltpu.get_barrier_semaphore()
        everyone = sorted(set(XZ + YC + XYC))
        for o in everyone:
            pl.semaphore_signal(barrier, inc=1, device_id=dev(o), device_id_type=MESH)

        pair = pair_ref[...]
        lane = lax.broadcasted_iota(jnp.int32, (1, B), 1)
        first = (lane < pair).astype(F32)
        up = (
            lax.broadcasted_iota(jnp.int32, (B, B), 0) < lax.broadcasted_iota(jnp.int32, (B, B), 1)
        ).astype(F32).astype(BF16)
        rank = dot(jnp.broadcast_to(first, (8, B)).astype(BF16), up)[0:1, :]
        slot = jnp.where(first > 0.5, rank, -1.0).astype(jnp.int32)
        top = (lax.broadcasted_iota(jnp.int32, (HB, B), 0) == slot).astype(F32).astype(BF16)
        partner = (lax.broadcasted_iota(jnp.int32, (B, B), 0) == pair).astype(F32).astype(BF16)
        perm[0:HB, :] = top
        perm[HB:B, :] = dot(top, partner).astype(BF16)
        ep[...] = dot(perm[...], emb_ref[...]).astype(BF16)
        uz, _ = unit(ep[...].astype(F32))
        zall[ix, ic] = uz.astype(BF16)

        load.wait()

        def norm_c(i, _):
            uc, _n = unit(praw[i].astype(F32))
            chat[pl.ds(pl.multiple_of(i * OB, OB), OB), :] = uc.astype(BF16)
            return 0

        lax.fori_loop(0, X * Z, norm_c, 0)

        def scores(h, fresh):
            rows = pl.ds(pl.multiple_of(h * B, B), B)
            zb = zall[ix, h]
            racc[rows, :] = jnp.zeros((B, 128), F32)

            def step(j, _):
                cols = pl.ds(pl.multiple_of(j * 256, 256), 256)
                e = jnp.exp(dot(zb, chat[cols, :], NT) * 10.0)
                E[rows, cols] = e
                k = e * e
                K[rows, cols] = k
                part = jnp.sum(k.reshape(B // 8, 8, 256), axis=0)
                colacc[:, cols] = part if fresh else colacc[:, cols] + part
                racc[rows, :] = racc[rows, :] + (e[:, :128] + e[:, 128:])
                return 0

            lax.fori_loop(0, NC // 256, step, 0)

        scores(ic, True)
        pl.semaphore_wait(barrier, len(everyone))
        send(zall.at[ix, ic], zall.at[ix, ic], core_s, core_r, (0, 0, 1, 0))
        take(zall.at[ix, 1 - ic], core_r)
        scores(1 - ic, False)

        def col_send(t):
            for j in range(CC):
                crow[j : j + 1, :] = jnp.sum(colacc[:, j * 128 : (j + 1) * 128], axis=0, keepdims=True)
            csend[t] = crow[...].astype(BF16)
            for i, o in enumerate(XZ):
                send(csend.at[t], crecv.at[t, i + 1], cs.at[t], cr.at[t], o)
            pltpu.make_async_copy(csend.at[t], crecv.at[t, 0], cr.at[t]).start()

        def col_take(t):
            take(crecv.at[t], cr.at[t])
            crow[...] = 1.0 / jnp.sum(crecv[t].astype(F32), axis=0)

        def row_pass(out, keep):
            def step(i, _):
                rows = pl.ds(pl.multiple_of(i * 128, 128), 128)
                acc = jnp.zeros((128, 128), F32)
                for j in range(CC):
                    w = K[rows, j * 128 : (j + 1) * 128] * crow[j : j + 1, :]
                    if keep:
                        K[rows, j * 128 : (j + 1) * 128] = w
                    acc = acc + w
                out[pl.ds(i, 1), :] = jnp.sum(acc.T, axis=0, keepdims=True)
                return 0

            lax.fori_loop(0, RC, step, 0)

        def col_pass():
            colacc[...] = jnp.zeros((8, NC), F32)

            def step(i, _):
                rows = pl.ds(pl.multiple_of(i * 128, 128), 128)
                r = rb[rows, :]
                for j in range(CC):
                    cols = slice(j * 128, (j + 1) * 128)
                    p = K[rows, cols] * r
                    colacc[:, cols] = colacc[:, cols] + jnp.sum(p.reshape(16, 8, 128), axis=0)
                return 0

            lax.fori_loop(0, RC, step, 0)

        def scores_t(lo, hi):
            def step(n, _):
                x, c, q = n // (C * B // 256), (n // (B // 256)) % C, n % (B // 256)
                zb = zall[x, c, pl.ds(pl.multiple_of(q * 256, 256), 256), :]
                mine = chat[pl.ds(pl.multiple_of(ix * TC, TC), TC), :]
                ET[:, pl.ds(pl.multiple_of(n * 256, 256), 256)] = jnp.exp(dot(mine, zb, NT) * 10.0)
                return 0

            lax.fori_loop(lo, hi, step, 0)

        col_send(0)
        for a in range(1, X):
            send(zall.at[ix, ic], zall.at[ix, ic], xs, xr.at[a], (a, 0, 0, 0))
        for i in range(RC):
            rsend1[RC + i : RC + i + 1, :] = jnp.sum(racc[i * 128 : (i + 1) * 128, :].T, axis=0, keepdims=True)
        permt[...] = perm[...].astype(F32).T.astype(BF16)
        col_take(0)
        row_pass(rsend1, False)
        for i, o in enumerate(YC):
            send(rsend1, rrecv1.at[i + 1], rs.at[0], rr.at[0], o)
        pltpu.make_async_copy(rsend1, rrecv1.at[0], rr.at[0]).start()
        take(rrecv1, rr.at[0])
        totals = jnp.sum(rrecv1[...], axis=0)
        rrow[...] = 1.0 / totals[:RC, :]
        rp4[ix] = 10.0 / totals[RC:, :]

        for i in range(RC):
            rb[i * 128 : (i + 1) * 128, :] = spread(rrow[i : i + 1, :])
        col_pass()
        col_send(1)
        for a in range(1, X):
            send(rp4.at[ix], rp4.at[ix], ps, pr.at[a], (a, 0, 0, 0))
        for a in range(1, X):
            src = (ix + X - a) % X
            take(zall.at[src, ic], xr.at[a])
            send(zall.at[src, ic], zall.at[src, ic], fs, fr.at[a], (0, 0, 1, 0))
        for i in range(RC):
            rpb[i * 128 : (i + 1) * 128, :] = spread(rp4[ix, i : i + 1, :])
        col_take(1)
        row_pass(rsend2, False)
        for i, o in enumerate(YC):
            send(rsend2, rrecv2.at[i + 1], rs.at[1], rr.at[1], o)
        pltpu.make_async_copy(rsend2, rrecv2.at[0], rr.at[1]).start()
        for a in range(1, X):
            take(zall.at[(ix + X - a) % X, 1 - ic], fr.at[a])
        NB = X * C * B // 256
        scores_t(0, NB // 2)
        take(rrecv2, rr.at[1])
        rrow[...] = 1.0 / jnp.sum(rrecv2[...], axis=0)

        for i in range(RC):
            rb[i * 128 : (i + 1) * 128, :] = spread(rrow[i : i + 1, :])
        col_pass()
        col_send(2)
        scores_t(NB // 2, NB)
        for a in range(1, X):
            take(rp4.at[(ix + X - a) % X], pr.at[a])
        col_take(2)
        row_pass(rsend3, True)
        YCI = {o: i + 1 for i, o in enumerate(YC)}
        YCI[(0, 0, 0, 0)] = 0
        for o in XYC:
            send(rsend3, rrecv3.at[ix * (len(YC) + 1) + YCI[(0,) + o[1:]]], rs.at[2], rr.at[2], o)
        pltpu.make_async_copy(rsend3, rrecv3.at[ix * (len(YC) + 1)], rr.at[2]).start()
        mine = crow[pl.ds(ix * (TC // 128), TC // 128), :]
        for i in range(TC // 128):
            c3b[i * 128 : (i + 1) * 128, :] = spread(mine[i : i + 1, :])

        def weigh(n, _):
            x = n // RC
            q = n % RC
            cols = pl.ds(pl.multiple_of(n * 128, 128), 128)
            e = ET[:, cols]
            WT[:, cols] = e * e * c3b[...]
            ET[:, cols] = e * rp4[x, pl.ds(q, 1), :]
            return 0

        lax.fori_loop(0, X * RC, weigh, 0)
        take(rrecv3, rr.at[2])
        for x in range(X):
            r34[x] = 10.0 / jnp.sum(rrecv3[x * (len(YC) + 1) : (x + 1) * (len(YC) + 1)], axis=0)
        for i in range(RC):
            rb[i * 128 : (i + 1) * 128, :] = spread(r34[ix, pl.ds(i, 1), :])

        def grad_r(i, _):
            ip = (i // BC) * BC + (i + BC // 2) % BC
            rows = pl.ds(pl.multiple_of(i * 128, 128), 128)
            prows = pl.ds(pl.multiple_of(ip * 128, 128), 128)
            rp, r3 = rpb[rows, :], rb[prows, :]
            for j in range(CC):
                cols = slice(j * 128, (j + 1) * 128)
                G[rows, cols] = (E[rows, cols] * rp - K[prows, cols] * r3).astype(BF16)
            return 0

        lax.fori_loop(0, RC, grad_r, 0)

        def mm_r(i, _):
            rows = pl.ds(pl.multiple_of(i * 256, 256), 256)
            gpart[rows, :] = dot(G[rows, :], chat[...])
            return 0

        lax.fori_loop(0, RT // 256, mm_r, 0)
        mine_rows = pl.ds(pl.multiple_of(ic * B, B), B)
        other_rows = pl.ds(pl.multiple_of((1 - ic) * B, B), B)
        ksend[...] = gpart[other_rows, :].astype(BF16)
        send(ksend, krecv, ks, kr, (0, 0, 1, 0))

        def grad_t(n, _):
            x, q = n // RC, n % RC
            qp = (q // BC) * BC + (q + BC // 2) % BC
            cols = pl.ds(pl.multiple_of(n * 128, 128), 128)
            pcols = pl.ds(pl.multiple_of((x * RC + qp) * 128, 128), 128)
            GT[:, cols] = (ET[:, cols] - WT[:, pcols] * r34[x, pl.ds(qp, 1), :]).astype(BF16)
            return 0

        lax.fori_loop(0, X * RC, grad_t, 0)
        zflat = zall[...].reshape(X * RT, D)

        def mm_t(i, _):
            rows = pl.ds(pl.multiple_of(i * 256, 256), 256)
            tpart[rows, :] = dot(GT[rows, :], zflat)
            return 0

        lax.fori_loop(0, TC // 256, mm_t, 0)
        zsend[...] = tpart[...].reshape(Z, OB, D).astype(BF16)
        for b in sorted(range(1, Z), key=lambda k: -ring(k, Z)):
            send(zsend.at[(iz + b) % Z], zrecv.at[b - 1], zs, zr, (0, b, 0, 0))

        take(krecv, kr)
        gpart[mine_rows, :] = gpart[mine_rows, :] + krecv[...].astype(F32)
        ysend[...] = gpart[mine_rows, :].reshape(Y, B // Y, D).astype(BF16)
        for f in sorted(range(1, Y), key=lambda k: -ring(k, Y)):
            send(ysend.at[(iy + f) % Y], yrecv.at[f - 1], ys, yr, (0, 0, 0, f))

        take(zrecv, zr)
        gcs = tpart[pl.ds(pl.multiple_of(iz * OB, OB), OB), :]
        gcs = gcs + jnp.sum(zrecv[...].astype(F32), axis=0)
        uc, nc = unit(praw[ix * Z + iz].astype(F32))
        gc_ref[...] = (gcs - uc * jnp.sum(uc * gcs, axis=1, keepdims=True)) / nc

        take(yrecv, yr)
        QB = B // Y
        gzs = gpart[pl.ds(pl.multiple_of(ic * B + iy * QB, QB), QB), :]
        gzs = gzs + jnp.sum(yrecv[...].astype(F32), axis=0)
        uq, nq = unit(ep[pl.ds(pl.multiple_of(iy * QB, QB), QB), :].astype(F32))
        yall[iy] = ((gzs - uq * jnp.sum(uq * gzs, axis=1, keepdims=True)) / nq).astype(BF16)
        for f in sorted(range(1, Y), key=lambda k: -ring(k, Y)):
            send(yall.at[iy], yall.at[iy], gs, gr, (0, 0, 0, f))
        take(yall.at[pl.ds(0, Y - 1)], gr)
        gz_ref[...] = dot(permt[...], yall[...].reshape(B, D))

        take(zall.at[ix, ic], core_s)
        take(zall.at[pl.ds(0, X - 1), 0], xs)
        take(zall.at[pl.ds(0, X - 1), 0], fs)
        take(rp4.at[pl.ds(0, X - 1)], ps)
        for t in range(3):
            take(crecv.at[t, pl.ds(0, len(XZ))], cs.at[t])
        take(rrecv1.at[pl.ds(0, len(YC))], rs.at[0])
        take(rrecv2.at[pl.ds(0, len(YC))], rs.at[1])
        take(rrecv3.at[pl.ds(0, len(XYC))], rs.at[2])
        take(ksend, ks)
        take(zrecv, zs)
        take(yrecv, ys)
        take(yall.at[pl.ds(0, Y - 1)], gs)

    V = pltpu.VMEM
    S = pltpu.SemaphoreType.DMA
    QB = B // Y
    scratch = [
        V((X * Z, OB, D), BF16),
        V((NC, D), BF16),
        V((B, D), BF16),
        V((B, B), BF16),
        V((B, B), BF16),
        V((X, C, B, D), BF16),
        V((RT, NC), F32),
        V((RT, NC), F32),
        V((TC, X * RT), F32),
        V((TC, X * RT), F32),
        V((RT, NC), BF16),
        V((TC, X * RT), BF16),
        V((8, NC), F32),
        V((RT, 128), F32),
        V((RT, 128), F32),
        V((RT, 128), F32),
        V((TC, 128), F32),
        V((CC, 128), F32),
        V((RC, 128), F32),
        V((X, RC, 128), F32),
        V((X, RC, 128), F32),
        V((3, CC, 128), BF16),
        V((3, len(XZ) + 1, CC, 128), BF16),
        V((2 * RC, 128), F32),
        V((len(YC) + 1, 2 * RC, 128), F32),
        V((RC, 128), F32),
        V((len(YC) + 1, RC, 128), F32),
        V((RC, 128), F32),
        V((X * (len(YC) + 1), RC, 128), F32),
        V((RT, D), F32),
        V((B, D), BF16),
        V((B, D), BF16),
        V((TC, D), F32),
        V((Z, OB, D), BF16),
        V((Z - 1, OB, D), BF16),
        V((Y, QB, D), BF16),
        V((Y - 1, QB, D), BF16),
        V((Y, QB, D), BF16),
        S((1,)),
        S, S,
        S, S((X,)),
        S, S((X,)),
        S((3,)), S((3,)),
        S((3,)), S((3,)),
        S, S((X,)),
        S, S,
        S, S,
        S, S,
        S, S,
    ]
    return kernel, scratch


def body(embeddings, prototypes, pair_index):
    B, D = embeddings.shape
    NCL = prototypes.shape[0]
    NC = NCL // C
    OB = NCL // (X * Z * C)
    kernel, scratch = make_kernel(B, D, NC)
    vm = pl.BlockSpec(memory_space=pltpu.VMEM)
    return pl.pallas_call(
        kernel,
        out_shape=(jax.ShapeDtypeStruct((B, D), F32), jax.ShapeDtypeStruct((OB, D), F32)),
        in_specs=[vm, pl.BlockSpec(memory_space=pl.ANY), vm],
        out_specs=(vm, vm),
        scratch_shapes=scratch,
        compiler_params=pltpu.CompilerParams(
            collective_id=0, has_side_effects=True, vmem_limit_bytes=60 * 2**20
        ),
        name="swav",
    )(embeddings, prototypes.reshape(X * Z, C, OB, D), pair_index.reshape(1, B))


def solution(mesh):
    return jax.shard_map(
        body,
        mesh=mesh,
        in_specs=(P("dp", None), P("proto", None), P("dp")),
        out_specs=(P("dp", None), P(("proto", "dp"), None)),
        check_vma=False,
    )
```

time: 1030 us -> 80.2 us (0.08)
  blocking collectives: 768 us -> 0 us
  waiting for transfers between devices: 132 us -> 0 us
  Pallas kernels: 0 us -> 75.8 us
  matrix products: 60.9 us -> 0 us
  other arithmetic: 28.7 us -> 0 us
  between operations: 15.6 us -> 0.64 us
  local copies, waits for them, and re-layouts: 17.5 us -> 3.34 us
    psum x6 -> x0, blocking collectives: 768 us -> none  [the longest x3 746 us: column_sum(): return lax.psum(local, 'dp')]
    reduce_scatter x1 -> x0, waiting for transfers between devices: 94.5 us -> none  [body(): lax.psum_scatter(lax.dot_general(affinity_derivative, z_hat, (((0,), (0,)...]
    pallas_call x0 -> x1, Pallas kernels: none -> 75.8 us  [body(): pl.pallas_call(kernel, out_shape=(jax.ShapeDtypeStruct((B, D), F32), jax....]
    dot_general x9 -> x0, matrix products: 60.9 us -> none  [the longest x3 30.5 us: body(): row_scale = 1.0 / row_sum(jnp.dot(kernel, col_scale, precision=hp))]
    psum x1 -> x0, waiting for transfers between devices: 37 us -> none  [body(): grad_zhat = lax.psum(grad_local, 'proto')]
    gather x1 -> x0, local copies, waits for them, and re-layouts: 12.2 us -> none  [body(): crossed_assignment = jnp.take(codes, pair_index, axis=0)]
  transfers between devices with their start and end apart: 2 -> 0, of which waited for: 2 -> 0; matrix products, arithmetic and copies ran while one was open for 1% -> 0% of each run, Pallas kernels for 0% -> 0%
where the time goes in v1:
time: 80.2 us; the launch traced here: 79.8 us
  Pallas kernels  75.8 us (95%)
  local copies, waits for them, and re-layouts  3.34 us (4%)
    pallas_call x1, Pallas kernels, body(): pl.pallas_call(kernel, out_shape=(jax.ShapeDtypeStruct((B, D), F32), jax....  75.8 us
    unnamed x2, local copies, waits for them, and re-layouts  3.34 us

profile of v1, /device:TPU:1, one launch (start us, length us, event | category | flops | bytes accessed | tf_op | source)
XLA Modules:
  0.0 79.8 jit_solution(18143497525527948826)
XLA Ops:
  0.6 75.8 %swav.1 = (f32[512,256]{1,0:T(8,128)}, f32[64,256]{1,0:T(8,128)}) custom-call(bf16[512,256]{1,0:T(8,128)(2,1)} %emb_ref.1, bf16[32,2,64,256]{3,2,1,0:T(8,128)(2,1)} %bitcast.2, s32[1,512]{1,0:T(1,128)} %bitcast.3), custom_call_target="tpu_custom_call" | custom-call | tf_op jit(solution)/shard_map/swav/pallas_call | solution.py:405
  76.5 1.9 %copy.7 = f32[512,256]{1,0:T(8,128)} copy(f32[512,256]{1,0:T(8,128)} %get-tuple-element.4) | data formatting | bytes 1048576
  78.3 1.5 %copy.8 = f32[64,256]{1,0:T(8,128)} copy(f32[64,256]{1,0:T(8,128)} %get-tuple-element.5) | data formatting | bytes 131072

commit v2 on v1

v2 whole, which is shorter than its diff:
```python
import jax
import jax.numpy as jnp
from jax import lax
from jax.experimental import pallas as pl
from jax.experimental.pallas import tpu as pltpu
from jax.sharding import PartitionSpec as P

X, Z, C, Y = 4, 8, 2, 4
MESH = pl.DeviceIdType.MESH
F32, BF16 = jnp.float32, jnp.bfloat16
NT = (((1,), (1,)), ((), ()))
NN = (((1,), (0,)), ((), ()))


def ring(k, n):
    return min(k, n - k)


def offsets(axes):
    span = [n if a in axes else 1 for a, n in zip("xzcy", (X, Z, C, Y))]
    out = [
        (a, b, e, f)
        for a in range(span[0])
        for b in range(span[1])
        for e in range(span[2])
        for f in range(span[3])
        if a or b or e or f
    ]
    out.sort(key=lambda t: -(4 * (ring(t[0], X) + ring(t[1], Z) + ring(t[3], Y)) + t[2]))
    return out


def dot(a, b, dims=NN):
    return lax.dot_general(a, b, dims, preferred_element_type=F32)


def unit(values):
    norm = jnp.sqrt(jnp.sum(values * values, axis=1, keepdims=True) + 1e-06)
    return values / norm, norm


def spread(row):
    return jnp.broadcast_to(row, (128, 128)).T


def make_kernel(B, D, NC):
    RT, RC, CC, TC = C * B, C * B // 128, NC // 128, NC // X
    OB = TC // Z
    BC = B // 128
    HB = B // 2
    FZ = sorted(range(Z), key=lambda k: -ring(k, Z))
    NEAR, FAR = (1, X - 1), 2
    XZ, YC, XYC = offsets("xz"), offsets("yc"), offsets("xyc")

    GR = len(YC) + 1
    YCI = {o: i + 1 for i, o in enumerate(YC)}
    YCI[(0, 0, 0, 0)] = 0

    def kernel(
        emb_ref, proto_ref, pair_ref, gz_ref, gc_ref,
        pair_v, emb_v, praw, chat, ep, perm, permt, zall, E, K, ET, WT, colacc, racc, rb, rpb, c3a, c3b, mine_c,
        crow, rrow, rp4, r34, csend, crecv, rsend1, rrecv1, rsend2, rrecv2, rsend3, rrecv3,
        gpart, ksend, krecv, tpart, zsend, zrecv, ysend, yrecv, yall,
        lsem, core_s, core_r, xs, xr, fs, fr, cs, cr, rs, rr, ps, pr, ks, kr, zs, zr, ys, yr, gs, gr,
    ):
        dp = lax.axis_index("dp")
        iy = lax.axis_index("proto")
        ix, iz, ic = dp // (Z * C), (dp // C) % Z, dp % C

        def dev(o):
            a, b, e, f = o
            nx = (ix + a) % X if a else ix
            nz = (iz + b) % Z if b else iz
            nc = (ic + e) % C if e else ic
            ny = (iy + f) % Y if f else iy
            return {"dp": (nx * Z + nz) * C + nc, "proto": ny}

        def send(src, dst, s, r, o):
            pltpu.make_async_remote_copy(
                src_ref=src, dst_ref=dst, send_sem=s, recv_sem=r, device_id=dev(o), device_id_type=MESH
            ).start()

        def take(ref, sem):
            pltpu.make_async_copy(ref, ref, sem).wait()

        loads = [
            pltpu.make_async_copy(pair_ref, pair_v, lsem.at[0]),
            pltpu.make_async_copy(emb_ref, emb_v, lsem.at[1]),
            pltpu.make_async_copy(proto_ref.at[:, ic], praw, lsem.at[2]),
        ]
        for load in loads:
            load.start()
        barrier = pltpu.get_barrier_semaphore()
        everyone = sorted(set(XZ + YC + XYC))
        for o in everyone:
            pl.semaphore_signal(barrier, inc=1, device_id=dev(o), device_id_type=MESH)

        loads[0].wait()
        pair = pair_v[...]
        lane = lax.broadcasted_iota(jnp.int32, (1, B), 1)
        first = (lane < pair).astype(F32)
        up = (
            lax.broadcasted_iota(jnp.int32, (B, B), 0) < lax.broadcasted_iota(jnp.int32, (B, B), 1)
        ).astype(F32).astype(BF16)
        rank = dot(jnp.broadcast_to(first, (8, B)).astype(BF16), up)[0:1, :]
        slot = jnp.where(first > 0.5, rank, -1.0).astype(jnp.int32)
        top = (lax.broadcasted_iota(jnp.int32, (HB, B), 0) == slot).astype(F32).astype(BF16)
        partner = (lax.broadcasted_iota(jnp.int32, (B, B), 0) == pair).astype(F32).astype(BF16)
        perm[0:HB, :] = top
        perm[HB:B, :] = dot(top, partner).astype(BF16)
        loads[1].wait()
        ep[...] = dot(perm[...], emb_v[...]).astype(BF16)
        uz, _ = unit(ep[...].astype(F32))
        zall[0, ic] = uz.astype(BF16)

        loads[2].wait()

        def norm_c(i, _):
            v = praw[pl.ds(i * (256 // OB), 256 // OB)].reshape(256, D).astype(F32)
            inv = 1.0 / jnp.sqrt(jnp.sum(v * v, axis=1, keepdims=True) + 1e-06)
            chat[pl.ds(pl.multiple_of(i * 256, 256), 256), :] = (v * inv).astype(BF16)
            return 0

        lax.fori_loop(0, NC // 256, norm_c, 0, unroll=2)

        def scores(h, js, fresh):
            rows = pl.ds(pl.multiple_of(h * B, B), B)
            zb = zall[0, h]
            for j in js:
                cols = slice(j * 256, (j + 1) * 256)
                e = jnp.exp(dot(zb, chat[cols, :], NT) * 10.0)
                E[rows, cols] = e
                k = e * e
                K[rows, cols] = k
                part = jnp.sum(k.reshape(B // 8, 8, 256), axis=0)
                colacc[:, cols] = part if fresh else colacc[:, cols] + part
                two = e[:, :128] + e[:, 128:]
                racc[rows, :] = two if j == 0 else racc[rows, :] + two

        NJ = NC // 256
        scores(ic, range(0, NJ - NJ // 4), True)
        pl.semaphore_wait(barrier, len(everyone))
        send(zall.at[0, ic], zall.at[0, ic], core_s, core_r, (0, 0, 1, 0))
        scores(ic, range(NJ - NJ // 4, NJ), True)
        take(zall.at[0, 1 - ic], core_r)
        scores(1 - ic, range(NJ), False)

        def col_send(t):
            for j in range(CC):
                crow[j : j + 1, :] = jnp.sum(colacc[:, j * 128 : (j + 1) * 128], axis=0, keepdims=True)
            csend[t] = crow[...].astype(BF16)
            for i, o in enumerate(XZ):
                send(csend.at[t], crecv.at[t, i + 1], cs.at[t], cr.at[t], o)
            pltpu.make_async_copy(csend.at[t], crecv.at[t, 0], cr.at[t]).start()

        def col_take(t):
            take(crecv.at[t], cr.at[t])
            crow[...] = 1.0 / jnp.sum(crecv[t].astype(F32), axis=0)

        def row_pass(out, keep):
            for i in range(RC):
                rows = slice(i * 128, (i + 1) * 128)
                acc = jnp.zeros((128, 128), F32)
                for j in range(CC):
                    w = K[rows, j * 128 : (j + 1) * 128] * crow[j : j + 1, :]
                    if keep:
                        K[rows, j * 128 : (j + 1) * 128] = w
                    acc = acc + w
                out[i : i + 1, :] = jnp.sum(acc.T, axis=0, keepdims=True)

        def col_pass():
            colacc[...] = jnp.zeros((8, NC), F32)

            def step(i, _):
                rows = pl.ds(pl.multiple_of(i * 128, 128), 128)
                r = rb[rows, :]
                for j in range(CC):
                    cols = slice(j * 128, (j + 1) * 128)
                    p = K[rows, cols] * r
                    colacc[:, cols] = colacc[:, cols] + jnp.sum(p.reshape(16, 8, 128), axis=0)
                return 0

            lax.fori_loop(0, RC, step, 0)

        def scores_t(a):
            mine = mine_c[...]
            for c in range(C):
                for q in range(B // 256):
                    n = (a * C + c) * (B // 256) + q
                    e = jnp.exp(dot(mine, zall[a, c, q * 256 : (q + 1) * 256, :], NT) * 10.0)
                    for half in range(2):
                        cols = slice(n * 256 + half * 128, n * 256 + (half + 1) * 128)
                        i = c * BC + q * 2 + half
                        eh = e[:, half * 128 : (half + 1) * 128]
                        WT[:, cols] = eh * eh
                        ET[:, cols] = eh * rp4[a, i : i + 1, :]

        def send_x(a):
            send(zall.at[0, ic], zall.at[a, ic], xs, xr.at[a], (a, 0, 0, 0))

        def forward(a):
            send(zall.at[a, ic], zall.at[a, ic], fs, fr.at[a], (0, 0, 1, 0))

        def relay(a, half):
            rows = pl.ds(half * HB, HB)
            send(zall.at[a, ic, rows], zall.at[FAR, ic, rows], xs, xr.at[FAR], (a, 0, 0, 0))

        col_send(0)
        for a in NEAR:
            send_x(a)
        for k, b in enumerate(FZ):
            mine_c[k * OB : (k + 1) * OB, :] = chat[pl.ds(pl.multiple_of(ix * TC + (iz + b) % Z * OB, OB), OB), :]
        for i in range(RC):
            rsend1[RC + i : RC + i + 1, :] = jnp.sum(racc[i * 128 : (i + 1) * 128, :].T, axis=0, keepdims=True)
        permt[...] = perm[...].astype(F32).T.astype(BF16)
        col_take(0)
        row_pass(rsend1, False)
        for i, o in enumerate(YC):
            send(rsend1, rrecv1.at[i + 1], rs.at[0], rr.at[0], o)
        pltpu.make_async_copy(rsend1, rrecv1.at[0], rr.at[0]).start()
        for half, a in enumerate(NEAR):
            take(zall.at[a, ic], xr.at[a])
            relay(a, half)
        for a in NEAR:
            forward(a)
        take(rrecv1, rr.at[0])
        totals = jnp.sum(rrecv1[...], axis=0)
        rrow[...] = 1.0 / totals[:RC, :]
        rp4[0] = 10.0 / totals[RC:, :]

        for i in range(RC):
            rb[i * 128 : (i + 1) * 128, :] = spread(rrow[i : i + 1, :])
        col_pass()
        col_send(1)
        for a in range(1, X):
            send(rp4.at[0], rp4.at[a], ps, pr.at[a], (a, 0, 0, 0))
        for i in range(RC):
            rpb[i * 128 : (i + 1) * 128, :] = spread(rp4[0, i : i + 1, :])
        scores_t(0)
        col_take(1)
        row_pass(rsend2, False)
        for i, o in enumerate(YC):
            send(rsend2, rrecv2.at[i + 1], rs.at[1], rr.at[1], o)
        pltpu.make_async_copy(rsend2, rrecv2.at[0], rr.at[1]).start()
        take(zall.at[FAR, ic], xr.at[FAR])
        forward(FAR)
        for a in NEAR:
            take(rp4.at[a], pr.at[a])
            take(zall.at[a, 1 - ic], fr.at[a])
            scores_t(a)
        take(rrecv2, rr.at[1])
        rrow[...] = 1.0 / jnp.sum(rrecv2[...], axis=0)

        for i in range(RC):
            rb[i * 128 : (i + 1) * 128, :] = spread(rrow[i : i + 1, :])
        col_pass()
        col_send(2)
        take(rp4.at[FAR], pr.at[FAR])
        take(zall.at[FAR, 1 - ic], fr.at[FAR])
        scores_t(FAR)
        col_take(2)
        row_pass(rsend3, True)
        for o in sorted(XYC, key=lambda o: o[0] != 0):
            send(rsend3, rrecv3.at[o[0] * GR + YCI[(0,) + o[1:]]], rs.at[2], rr.at[3 if o[0] else 2], o)
        pltpu.make_async_copy(rsend3, rrecv3.at[0], rr.at[2]).start()
        mine = crow[pl.ds(ix * (TC // 128), TC // 128), :]
        for i in range(TC // 128):
            c3a[i * 128 : (i + 1) * 128, :] = spread(mine[i : i + 1, :])
        for k, b in enumerate(FZ):
            c3b[k * OB : (k + 1) * OB, :] = c3a[pl.ds(pl.multiple_of((iz + b) % Z * OB, OB), OB), :]
        c3 = c3b[...]
        for n in range(X * RC):
            cols = slice(n * 128, (n + 1) * 128)
            WT[:, cols] = WT[:, cols] * c3
        take(rrecv3.at[pl.ds(0, GR)], rr.at[2])
        r34[0] = 10.0 / jnp.sum(rrecv3[0:GR], axis=0)
        for i in range(RC):
            rb[i * 128 : (i + 1) * 128, :] = spread(r34[0, i : i + 1, :])

        def grad_r(h):
            for q in range(2):
                rows = pl.ds(pl.multiple_of(h * B + q * HB, HB), HB)
                prows = pl.ds(pl.multiple_of(h * B + (1 - q) * HB, HB), HB)
                rp, r3 = rpb[rows, :], rb[prows, :]
                g = [
                    (E[rows, j * 128 : (j + 1) * 128] * rp - K[prows, j * 128 : (j + 1) * 128] * r3).astype(BF16)
                    for j in range(CC)
                ]
                yield q, dot(jnp.concatenate(g, axis=1), chat[...])

        for q, part in grad_r(1 - ic):
            ksend[q] = part.astype(BF16)
        for q in range(2):
            send(ksend.at[q], krecv.at[q], ks.at[q], kr.at[q], (0, 0, 1, 0))
        for q, part in grad_r(ic):
            gpart[q] = part
        far_y = sorted(range(1, Y), key=lambda k: -ring(k, Y))
        for q in range(2):
            take(krecv.at[q], kr.at[q])
            gpart[q] = gpart[q] + krecv[q].astype(F32)
            ysend[q] = gpart[q].reshape(Y, HB // Y, D).astype(BF16)
            for f in far_y:
                send(ysend.at[q, (iy + f) % Y], yrecv.at[q, f - 1], ys.at[q], yr.at[q], (0, 0, 0, f))

        take(rrecv3.at[pl.ds(GR, (X - 1) * GR)], rr.at[3])
        for a in range(1, X):
            r34[a] = 10.0 / jnp.sum(rrecv3[a * GR : (a + 1) * GR], axis=0)
        for n in range(X * C):
            a, c = n // C, n % C
            g = []
            for q in range(BC):
                qp = (q + BC // 2) % BC
                cols = slice(n * B + q * 128, n * B + (q + 1) * 128)
                pcols = slice(n * B + qp * 128, n * B + (qp + 1) * 128)
                r3 = r34[a, c * BC + qp : c * BC + qp + 1, :]
                g.append((ET[:, cols] - WT[:, pcols] * r3).astype(BF16))
            part = dot(jnp.concatenate(g, axis=1), zall[a, c])
            tpart[...] = part if n == 0 else tpart[...] + part
        zsend[...] = tpart[0 : (Z - 1) * OB, :].reshape(Z - 1, OB, D).astype(BF16)
        for k in range(Z - 1):
            send(zsend.at[k], zrecv.at[k], zs, zr, (0, FZ[k], 0, 0))

        SB = HB // Y
        for q in range(2):
            take(yrecv.at[q], yr.at[q])
            at = pl.ds(pl.multiple_of(iy * SB, SB), SB)
            gzs = gpart[q, at, :] + jnp.sum(yrecv[q].astype(F32), axis=0)
            uq, nq = unit(ep[pl.ds(pl.multiple_of(q * HB + iy * SB, SB), SB), :].astype(F32))
            yall[q, iy] = ((gzs - uq * jnp.sum(uq * gzs, axis=1, keepdims=True)) / nq).astype(BF16)
            for f in far_y:
                send(yall.at[q, iy], yall.at[q, iy], gs.at[q], gr.at[q], (0, 0, 0, f))

        take(zrecv, zr)
        gcs = tpart[(Z - 1) * OB : Z * OB, :] + jnp.sum(zrecv[...].astype(F32), axis=0)
        uc, nc = unit(praw[ix * Z + iz].astype(F32))
        gc_ref[...] = (gcs - uc * jnp.sum(uc * gcs, axis=1, keepdims=True)) / nc
        for q in range(2):
            take(yall.at[q, pl.ds(0, Y - 1)], gr.at[q])
        gz_ref[...] = dot(permt[...], yall[...].reshape(B, D))

        take(zall.at[0, ic], core_s)
        take(zall.at[pl.ds(0, X - 1), 0], xs)
        take(zall.at[pl.ds(0, X - 1), 0], fs)
        take(rp4.at[pl.ds(0, X - 1)], ps)
        for t in range(3):
            take(crecv.at[t, pl.ds(0, len(XZ))], cs.at[t])
        take(rrecv1.at[pl.ds(0, len(YC))], rs.at[0])
        take(rrecv2.at[pl.ds(0, len(YC))], rs.at[1])
        take(rrecv3.at[pl.ds(0, len(XYC))], rs.at[2])
        take(zrecv, zs)
        for q in range(2):
            take(ksend.at[q], ks.at[q])
            take(yrecv.at[q], ys.at[q])
            take(yall.at[q, pl.ds(0, Y - 1)], gs.at[q])

    V = pltpu.VMEM
    S = pltpu.SemaphoreType.DMA
    scratch = [
        V((1, B), jnp.int32),
        V((B, D), BF16),
        V((X * Z, OB, D), BF16),
        V((NC, D), BF16),
        V((B, D), BF16),
        V((B, B), BF16),
        V((B, B), BF16),
        V((X, C, B, D), BF16),
        V((RT, NC), F32),
        V((RT, NC), F32),
        V((TC, X * RT), F32),
        V((TC, X * RT), F32),
        V((8, NC), F32),
        V((RT, 128), F32),
        V((RT, 128), F32),
        V((RT, 128), F32),
        V((TC, 128), F32),
        V((TC, 128), F32),
        V((TC, D), BF16),
        V((CC, 128), F32),
        V((RC, 128), F32),
        V((X, RC, 128), F32),
        V((X, RC, 128), F32),
        V((3, CC, 128), BF16),
        V((3, len(XZ) + 1, CC, 128), BF16),
        V((2 * RC, 128), F32),
        V((len(YC) + 1, 2 * RC, 128), F32),
        V((RC, 128), F32),
        V((len(YC) + 1, RC, 128), F32),
        V((RC, 128), F32),
        V((X * (len(YC) + 1), RC, 128), F32),
        V((2, HB, D), F32),
        V((2, HB, D), BF16),
        V((2, HB, D), BF16),
        V((TC, D), F32),
        V((Z - 1, OB, D), BF16),
        V((Z - 1, OB, D), BF16),
        V((2, Y, HB // Y, D), BF16),
        V((2, Y - 1, HB // Y, D), BF16),
        V((2, Y, HB // Y, D), BF16),
        S((3,)),
        S, S,
        S, S((X,)),
        S, S((X,)),
        S((3,)), S((3,)),
        S((3,)), S((4,)),
        S, S((X,)),
        S((2,)), S((2,)),
        S, S,
        S((2,)), S((2,)),
        S((2,)), S((2,)),
    ]
    return kernel, scratch


def place(gz_ref, gc_ref, gz_out, gc_out):
    gz_out[...] = gz_ref[...]
    gc_out[...] = gc_ref[...]


def body(embeddings, prototypes, pair_index):
    B, D = embeddings.shape
    NCL = prototypes.shape[0]
    NC = NCL // C
    OB = NCL // (X * Z * C)
    kernel, scratch = make_kernel(B, D, NC)
    vm = pl.BlockSpec(memory_space=pltpu.VMEM)
    hbm = pl.BlockSpec(memory_space=pl.ANY)
    shapes = (jax.ShapeDtypeStruct((B, D), F32), jax.ShapeDtypeStruct((OB, D), F32))
    grads = pl.pallas_call(
        kernel,
        out_shape=shapes,
        in_specs=[hbm, hbm, hbm],
        out_specs=(vm, vm),
        scratch_shapes=scratch,
        compiler_params=pltpu.CompilerParams(
            collective_id=0, has_side_effects=True, vmem_limit_bytes=60 * 2**20
        ),
        name="swav",
    )(embeddings, prototypes.reshape(X * Z, C, OB, D), pair_index.reshape(1, B))
    return pl.pallas_call(
        place,
        out_shape=shapes,
        in_specs=[vm, vm],
        out_specs=(vm, vm),
        name="place",
    )(*grads)


def solution(mesh):
    return jax.shard_map(
        body,
        mesh=mesh,
        in_specs=(P("dp", None), P("proto", None), P("dp")),
        out_specs=(P("dp", None), P(("proto", "dp"), None)),
        check_vma=False,
    )
```

time: 80.2 us -> 64.4 us (0.80)
  Pallas kernels: 75.8 us -> 63.7 us
  local copies, waits for them, and re-layouts: 3.34 us -> 0 us
    pallas_call x1 -> x2, Pallas kernels: 75.8 us -> 63.7 us  [the longest x1 61.8 us: body(): pl.pallas_call(kernel, out_shape=shapes, in_specs=[hbm, hbm, hbm], out_sp...]
    unnamed x2 -> x0, local copies, waits for them, and re-layouts: 3.34 us -> none
where the time goes in v2:
time: 64.4 us; the launch traced here: 64.3 us
  Pallas kernels  63.7 us (99%)
    pallas_call x1, Pallas kernels, body(): pl.pallas_call(kernel, out_shape=shapes, in_specs=[hbm, hbm, hbm], out_sp...  61.8 us
    pallas_call x1, Pallas kernels, body(): pl.pallas_call(place, out_shape=shapes, in_specs=[vm, vm], out_specs=(vm,...  1.88 us

profile of v2, /device:TPU:1, one launch (start us, length us, event | category | flops | bytes accessed | tf_op | source)
XLA Modules:
  0.0 64.3 jit_solution(16052438942799916139)
XLA Ops:
  0.6 61.8 %swav.1 = (f32[512,256]{1,0:T(8,128)}, f32[64,256]{1,0:T(8,128)}) custom-call(bf16[512,256]{1,0:T(8,128)(2,1)} %emb_ref.1, bf16[32,2,64,256]{3,2,1,0:T(8,128)(2,1)} %bitcast.2, s32[1,512]{1,0:T(1,128)} %bitcast.3), custom_call_target="tpu_custom_call" | custom-call | tf_op jit(solution)/shard_map/swav/pallas_call | solution.py:428
  62.4 1.9 %place.1 = (f32[512,256]{1,0:T(8,128)}, f32[64,256]{1,0:T(8,128)}) custom-call(f32[512,256]{1,0:T(8,128)} %get-tuple-element.4.gz_ref, f32[64,256]{1,0:T(8,128)} %get-tuple-element.5.gc_ref), custom_call_target="tpu_custom_call" | custom-call | tf_op jit(solution)/shard_map/place/pallas_call | solution.py:439

commit v3 on v2

v3 whole, which is shorter than its diff:
```python
import jax
import jax.numpy as jnp
from jax import lax
from jax.experimental import pallas as pl
from jax.experimental.pallas import tpu as pltpu
from jax.sharding import PartitionSpec as P

X, Z, C, Y = 4, 8, 2, 4
MESH = pl.DeviceIdType.MESH
F32, BF16 = jnp.float32, jnp.bfloat16
NT = (((1,), (1,)), ((), ()))
NN = (((1,), (0,)), ((), ()))


def ring(k, n):
    return min(k, n - k)


def offsets(axes):
    span = [n if a in axes else 1 for a, n in zip("xzcy", (X, Z, C, Y))]
    out = [
        (a, b, e, f)
        for a in range(span[0])
        for b in range(span[1])
        for e in range(span[2])
        for f in range(span[3])
        if a or b or e or f
    ]
    return sorted(out, key=farthest)


def farthest(t):
    return -(4 * (ring(t[0], X) + ring(t[1], Z) + ring(t[3], Y)) + t[2])


def dot(a, b, dims=NN):
    return lax.dot_general(a, b, dims, preferred_element_type=F32)


def unit(values):
    norm = jnp.sqrt(jnp.sum(values * values, axis=1, keepdims=True) + 1e-06)
    return values / norm, norm


def spread(row):
    return jnp.broadcast_to(row, (128, 128)).T


def make_kernel(B, D, NC):
    RT, RC, CC, TC = C * B, C * B // 128, NC // 128, NC // X
    OB = TC // Z
    BC = B // 128
    HB = B // 2
    FZ = [Z // 2 + k // 2 if k % 2 == 0 else Z // 2 - (k + 1) // 2 for k in range(Z)]
    NEAR, FAR = (1, X - 1), 2
    XZ, YC, XYC = offsets("xz"), offsets("yc"), offsets("xyc")

    GR = len(YC) + 1
    YCI = {o: i + 1 for i, o in enumerate(YC)}
    YCI[(0, 0, 0, 0)] = 0

    def kernel(
        emb_ref, proto_ref, pair_ref, gz_ref, gc_ref,
        pair_v, emb_v, zu, praw, chat, chato, ep, perm, permt, zall, E, K, ET, WT, colacc, racc, rb, rpb, c3a, c3b, mine_c,
        crow, rrow, rp4, r34, csend, crecv, fsend, frecv, tsend, trecv, rsend, rrecv, rsend3, rrecv3,
        gpart, ksend, krecv, tpart, zsend, zrecv, ysend, yrecv, yall,
        lsem, core_s, core_r, xs, xr, fs, fr, cs, cr, f_s, f_r, ts, tr, rs, rr, ps, pr, ks, kr, zs, zr, ys, yr, gs, gr,
    ):
        dp = lax.axis_index("dp")
        iy = lax.axis_index("proto")
        ix, iz, ic = dp // (Z * C), (dp // C) % Z, dp % C

        def dev(o):
            a, b, e, f = o
            nx = (ix + a) % X if a else ix
            nz = (iz + b) % Z if b else iz
            nc = (ic + e) % C if e else ic
            ny = (iy + f) % Y if f else iy
            return {"dp": (nx * Z + nz) * C + nc, "proto": ny}

        def send(src, dst, s, r, o):
            pltpu.make_async_remote_copy(
                src_ref=src, dst_ref=dst, send_sem=s, recv_sem=r, device_id=dev(o), device_id_type=MESH
            ).start()

        def take(ref, sem):
            pltpu.make_async_copy(ref, ref, sem).wait()

        loads = [
            pltpu.make_async_copy(pair_ref, pair_v, lsem.at[0]),
            pltpu.make_async_copy(emb_ref, emb_v, lsem.at[1]),
            pltpu.make_async_copy(proto_ref, praw, lsem.at[2]),
        ]
        for load in loads:
            load.start()
        barrier = pltpu.get_barrier_semaphore()
        everyone = sorted(sorted(set(XZ + YC + XYC)), key=farthest)
        for o in everyone:
            pl.semaphore_signal(barrier, inc=1, device_id=dev(o), device_id_type=MESH)

        loads[1].wait()
        loads[0].wait()
        v = emb_v[...].astype(F32)
        zu[...] = (v * (1.0 / jnp.sqrt(jnp.sum(v * v, axis=1, keepdims=True) + 1e-06))).astype(BF16)
        loads[2].wait()
        NB = 256 // OB

        def norm_c(half, out):
            def step(i, _):
                v = praw[pl.ds(i * NB, NB), half].reshape(256, D).astype(F32)
                inv = 1.0 / jnp.sqrt(jnp.sum(v * v, axis=1, keepdims=True) + 1e-06)
                out[pl.ds(pl.multiple_of(i * 256, 256), 256), :] = (v * inv).astype(BF16)
                return 0

            lax.fori_loop(0, NC // 256, step, 0, unroll=2)

        def first_totals(prototypes, out):
            zb = zu[...]
            for j in range(NC // 256):
                k = jnp.exp(dot(zb, prototypes[j * 256 : (j + 1) * 256, :], NT) * 20.0)
                colacc[:, j * 256 : (j + 1) * 256] = jnp.sum(k.reshape(B // 8, 8, 256), axis=0)
            for j in range(CC):
                out[j : j + 1, :] = jnp.sum(colacc[:, j * 128 : (j + 1) * 128], axis=0, keepdims=True)

        norm_c(1 - ic, chato)
        norm_c(ic, chat)
        first_totals(chato, fsend)
        pl.semaphore_wait(barrier, len(everyone))
        send(fsend, frecv, f_s, f_r, (0, 0, 1, 0))
        first_totals(chat, crow)

        def reorder():
            pair = pair_v[...]
            lane = lax.broadcasted_iota(jnp.int32, (1, B), 1)
            first = (lane < pair).astype(F32)
            up = (
                lax.broadcasted_iota(jnp.int32, (B, B), 0) < lax.broadcasted_iota(jnp.int32, (B, B), 1)
            ).astype(F32).astype(BF16)
            rank = dot(jnp.broadcast_to(first, (8, B)).astype(BF16), up)[0:1, :]
            slot = jnp.where(first > 0.5, rank, -1.0).astype(jnp.int32)
            top = (lax.broadcasted_iota(jnp.int32, (HB, B), 0) == slot).astype(F32).astype(BF16)
            partner = (lax.broadcasted_iota(jnp.int32, (B, B), 0) == pair).astype(F32).astype(BF16)
            perm[0:HB, :] = top
            perm[HB:B, :] = dot(top, partner).astype(BF16)
            ep[...] = dot(perm[...], emb_v[...]).astype(BF16)
            uz, _ = unit(ep[...].astype(F32))
            zall[0, ic] = uz.astype(BF16)

        def scores(h, js):
            rows = pl.ds(pl.multiple_of(h * B, B), B)
            zb = zall[0, h]
            for j in js:
                cols = slice(j * 256, (j + 1) * 256)
                e = jnp.exp(dot(zb, chat[cols, :], NT) * 10.0)
                E[rows, cols] = e
                k = e * e
                K[rows, cols] = k
                two = e[:, :128] + e[:, 128:]
                racc[rows, :] = two if j == 0 else racc[rows, :] + two

        def col_send(t):
            if t:
                for j in range(CC):
                    crow[j : j + 1, :] = jnp.sum(colacc[:, j * 128 : (j + 1) * 128], axis=0, keepdims=True)
            csend[t] = crow[...].astype(BF16)
            for i, o in enumerate(XZ):
                send(csend.at[t], crecv.at[t, i + 1], cs.at[t], cr.at[t], o)
            pltpu.make_async_copy(csend.at[t], crecv.at[t, 0], cr.at[t]).start()

        def col_take(t):
            take(crecv.at[t], cr.at[t])
            crow[...] = 1.0 / jnp.sum(crecv[t].astype(F32), axis=0)

        def row_pass(out, blocks, keep):
            for i in range(blocks[0] * BC, (blocks[-1] + 1) * BC):
                rows = slice(i * 128, (i + 1) * 128)
                acc = jnp.zeros((128, 128), F32)
                for j in range(CC):
                    w = K[rows, j * 128 : (j + 1) * 128] * crow[j : j + 1, :]
                    if keep:
                        K[rows, j * 128 : (j + 1) * 128] = w
                    acc = acc + w
                out[i // BC, i % BC : i % BC + 1, :] = jnp.sum(acc.T, axis=0, keepdims=True)

        def col_pass(t):
            for blk in range(C):
                take(rrecv.at[t, blk], rr.at[t * C + blk])
                rrow[...] = 1.0 / jnp.sum(rrecv[t, blk], axis=0)
                for i in range(BC):
                    rb[i * 128 : (i + 1) * 128, :] = spread(rrow[i : i + 1, :])

                for jg in range(0, CC, 8):
                    acc = [jnp.zeros((8, 128), F32) for _ in range(8)]
                    for i in range(BC):
                        r = rb[i * 128 : (i + 1) * 128, :]
                        rows = slice(blk * B + i * 128, blk * B + (i + 1) * 128)
                        for j in range(8):
                            p = K[rows, (jg + j) * 128 : (jg + j + 1) * 128] * r
                            acc[j] = acc[j] + jnp.sum(p.reshape(16, 8, 128), axis=0)
                    for j in range(8):
                        cols = slice((jg + j) * 128, (jg + j + 1) * 128)
                        colacc[:, cols] = colacc[:, cols] + acc[j] if blk else acc[j]

        def row_send(t):
            for blk in range(C):
                row_pass(rsend.at[t], (blk,), False)
                for i, o in enumerate(YC):
                    send(rsend.at[t, blk], rrecv.at[t, blk, i + 1], rs.at[t * C + blk], rr.at[t * C + blk], o)
                pltpu.make_async_copy(rsend.at[t, blk], rrecv.at[t, blk, 0], rr.at[t * C + blk]).start()

        def scores_t(a):
            mine = mine_c[...]
            for c in range(C):
                for q in range(B // 256):
                    n = (a * C + c) * (B // 256) + q
                    e = jnp.exp(dot(mine, zall[a, c, q * 256 : (q + 1) * 256, :], NT) * 10.0)
                    for half in range(2):
                        cols = slice(n * 256 + half * 128, n * 256 + (half + 1) * 128)
                        i = c * BC + q * 2 + half
                        eh = e[:, half * 128 : (half + 1) * 128]
                        WT[:, cols] = eh * eh
                        ET[:, cols] = eh * rp4[a, i : i + 1, :]

        def send_x(a):
            send(zall.at[0, ic], zall.at[a, ic], xs, xr.at[a], (a, 0, 0, 0))

        def forward(a):
            send(zall.at[a, ic], zall.at[a, ic], fs, fr.at[a], (0, 0, 1, 0))

        def relay(a, half):
            rows = pl.ds(half * HB, HB)
            send(zall.at[a, ic, rows], zall.at[FAR, ic, rows], xs, xr.at[FAR], (a, 0, 0, 0))

        take(frecv, f_r)
        crow[...] = crow[...] + frecv[...]
        col_send(0)
        reorder()
        send(zall.at[0, ic], zall.at[0, ic], core_s, core_r, (0, 0, 1, 0))
        for a in NEAR:
            send_x(a)
        scores(ic, range(NC // 256))
        take(zall.at[0, 1 - ic], core_r)
        scores(1 - ic, range(NC // 256))
        for i in range(RC):
            tsend[i : i + 1, :] = jnp.sum(racc[i * 128 : (i + 1) * 128, :].T, axis=0, keepdims=True)
        for i, o in enumerate(YC):
            send(tsend, trecv.at[i + 1], ts, tr, o)
        pltpu.make_async_copy(tsend, trecv.at[0], tr).start()
        col_take(0)
        row_send(0)
        permt[...] = perm[...].astype(F32).T.astype(BF16)
        for k, b in enumerate(FZ):
            mine_c[k * OB : (k + 1) * OB, :] = chat[pl.ds(pl.multiple_of(ix * TC + (iz + b) % Z * OB, OB), OB), :]
        take(trecv, tr)
        rp4[0] = 10.0 / jnp.sum(trecv[...], axis=0)
        for a in range(1, X):
            send(rp4.at[0], rp4.at[a], ps, pr.at[a], (a, 0, 0, 0))
        for half, a in enumerate(NEAR):
            take(zall.at[a, ic], xr.at[a])
            relay(a, half)
        for a in NEAR:
            forward(a)

        col_pass(0)
        col_send(1)
        for i in range(RC):
            rpb[i * 128 : (i + 1) * 128, :] = spread(rp4[0, i : i + 1, :])

        def scale(i, _):
            rows = pl.ds(pl.multiple_of(i * 64, 64), 64)
            rp = rpb[rows, :]
            for j in range(CC):
                E[rows, j * 128 : (j + 1) * 128] = E[rows, j * 128 : (j + 1) * 128] * rp
            return 0

        lax.fori_loop(0, RT // 64, scale, 0)
        scores_t(0)
        col_take(1)
        row_send(1)
        take(zall.at[FAR, ic], xr.at[FAR])
        forward(FAR)
        for a in NEAR:
            take(rp4.at[a], pr.at[a])
            take(zall.at[a, 1 - ic], fr.at[a])
            scores_t(a)

        col_pass(1)
        col_send(2)
        take(rp4.at[FAR], pr.at[FAR])
        take(zall.at[FAR, 1 - ic], fr.at[FAR])
        scores_t(FAR)
        col_take(2)
        row_pass(rsend3, range(C), True)
        for o in sorted(XYC, key=lambda o: o[0] != 0):
            send(rsend3, rrecv3.at[o[0] * GR + YCI[(0,) + o[1:]]], rs.at[4], rr.at[5 if o[0] else 4], o)
        pltpu.make_async_copy(rsend3, rrecv3.at[0], rr.at[4]).start()
        mine = crow[pl.ds(ix * (TC // 128), TC // 128), :]
        for i in range(TC // 128):
            c3a[i * 128 : (i + 1) * 128, :] = spread(mine[i : i + 1, :])
        for k, b in enumerate(FZ):
            c3b[k * OB : (k + 1) * OB, :] = c3a[pl.ds(pl.multiple_of((iz + b) % Z * OB, OB), OB), :]
        c3 = c3b[...]
        for n in range(X * RC):
            cols = slice(n * 128, (n + 1) * 128)
            WT[:, cols] = WT[:, cols] * c3
        take(rrecv3.at[pl.ds(0, GR)], rr.at[4])
        r34[0] = 10.0 / jnp.sum(rrecv3[0:GR], axis=0).reshape(RC, 128)
        for i in range(RC):
            rb[i * 128 : (i + 1) * 128, :] = spread(r34[0, i : i + 1, :])

        def grad_r(h, out):
            for q in range(2):
                rows = pl.ds(pl.multiple_of(h * B + q * HB, HB), HB)
                prows = pl.ds(pl.multiple_of(h * B + (1 - q) * HB, HB), HB)
                r3 = rb[prows, :]
                g = [
                    (E[rows, j * 128 : (j + 1) * 128] - K[prows, j * 128 : (j + 1) * 128] * r3).astype(BF16)
                    for j in range(CC)
                ]
                out[q] = dot(jnp.concatenate(g, axis=1), chat[...]).astype(out.dtype)

        grad_r(1 - ic, ksend)
        for q in range(2):
            send(ksend.at[q], krecv.at[q], ks.at[q], kr.at[q], (0, 0, 1, 0))
        grad_r(ic, gpart)
        take(rrecv3.at[pl.ds(GR, (X - 1) * GR)], rr.at[5])
        for a in range(1, X):
            r34[a] = 10.0 / jnp.sum(rrecv3[a * GR : (a + 1) * GR], axis=0).reshape(RC, 128)
        far_y = sorted(range(1, Y), key=lambda k: -ring(k, Y))
        for q in range(2):
            take(krecv.at[q], kr.at[q])
            gpart[q] = gpart[q] + krecv[q].astype(F32)
            ysend[q] = gpart[q].reshape(Y, HB // Y, D).astype(BF16)
            for f in far_y:
                send(ysend.at[q, (iy + f) % Y], yrecv.at[q, f - 1], ys.at[q], yr.at[q], (0, 0, 0, f))

        HT, ZH = TC // 2, Z // 2

        def grad_t(m, _):
            rows = pl.ds(pl.multiple_of(m * HT, HT), HT)
            g = []
            for n in range(X * RC):
                a, q = n // RC, n % RC
                qp = q // BC * BC + (q + BC // 2) % BC
                cols, pcols = slice(n * 128, (n + 1) * 128), slice((a * RC + qp) * 128, (a * RC + qp + 1) * 128)
                g.append((ET[rows, cols] - WT[rows, pcols] * r34[a, qp : qp + 1, :]).astype(BF16))
            part = dot(jnp.concatenate(g, axis=1), zall[...].reshape(X * RT, D))
            tpart[rows, :] = part
            zsend[pl.ds(m * ZH, ZH)] = part.reshape(ZH, OB, D).astype(BF16)
            for k in range(ZH):
                b = Z // 2 + m * (ZH // 2) + k // 2 if k % 2 == 0 else Z // 2 - m * (ZH // 2) - (k + 1) // 2
                to = {"dp": (ix * Z + (iz + b) % Z) * C + ic, "proto": iy}

                def go(k=k, to=to):
                    pltpu.make_async_remote_copy(
                        src_ref=zsend.at[m * ZH + k], dst_ref=zrecv.at[m * ZH + k], send_sem=zs, recv_sem=zr,
                        device_id=to, device_id_type=MESH,
                    ).start()

                if k < ZH - 1:
                    go()
                else:
                    pl.when(m == 0)(go)
            return 0

        lax.fori_loop(0, 2, grad_t, 0)

        SB = HB // Y
        for q in range(2):
            take(yrecv.at[q], yr.at[q])
            at = pl.ds(pl.multiple_of(iy * SB, SB), SB)
            gzs = gpart[q, at, :] + jnp.sum(yrecv[q].astype(F32), axis=0)
            uq, nq = unit(ep[pl.ds(pl.multiple_of(q * HB + iy * SB, SB), SB), :].astype(F32))
            yall[q, iy] = ((gzs - uq * jnp.sum(uq * gzs, axis=1, keepdims=True)) / nq).astype(BF16)
            for f in far_y:
                send(yall.at[q, iy], yall.at[q, iy], gs.at[q], gr.at[q], (0, 0, 0, f))

        take(zrecv, zr)
        gcs = tpart[(Z - 1) * OB : Z * OB, :] + jnp.sum(zrecv[...].astype(F32), axis=0)
        uc, nc = unit(praw[ix * Z + iz, ic].astype(F32))
        gc_ref[...] = (gcs - uc * jnp.sum(uc * gcs, axis=1, keepdims=True)) / nc
        for q in range(2):
            take(yall.at[q, pl.ds(0, Y - 1)], gr.at[q])
        gz_ref[...] = dot(permt[...], yall[...].reshape(B, D))

        take(zall.at[0, ic], core_s)
        take(zall.at[pl.ds(0, X - 1), 0], xs)
        take(zall.at[pl.ds(0, X - 1), 0], fs)
        take(rp4.at[pl.ds(0, X - 1)], ps)
        for t in range(3):
            take(crecv.at[t, pl.ds(0, len(XZ))], cs.at[t])
        take(fsend, f_s)
        take(trecv.at[pl.ds(0, len(YC))], ts)
        for t in range(2):
            for blk in range(C):
                take(rrecv.at[t, blk, pl.ds(0, len(YC))], rs.at[t * C + blk])
        take(rrecv3.at[pl.ds(0, len(XYC))], rs.at[4])
        take(zrecv, zs)
        for q in range(2):
            take(ksend.at[q], ks.at[q])
            take(yrecv.at[q], ys.at[q])
            take(yall.at[q, pl.ds(0, Y - 1)], gs.at[q])

    V = pltpu.VMEM
    S = pltpu.SemaphoreType.DMA
    scratch = [
        V((1, B), jnp.int32),
        V((B, D), BF16),
        V((B, D), BF16),
        V((X * Z, C, OB, D), BF16),
        V((NC, D), BF16),
        V((NC, D), BF16),
        V((B, D), BF16),
        V((B, B), BF16),
        V((B, B), BF16),
        V((X, C, B, D), BF16),
        V((RT, NC), F32),
        V((RT, NC), F32),
        V((TC, X * RT), F32),
        V((TC, X * RT), F32),
        V((8, NC), F32),
        V((RT, 128), F32),
        V((RT, 128), F32),
        V((RT, 128), F32),
        V((TC, 128), F32),
        V((TC, 128), F32),
        V((TC, D), BF16),
        V((CC, 128), F32),
        V((BC, 128), F32),
        V((X, RC, 128), F32),
        V((X, RC, 128), F32),
        V((3, CC, 128), BF16),
        V((3, len(XZ) + 1, CC, 128), BF16),
        V((CC, 128), F32),
        V((CC, 128), F32),
        V((RC, 128), F32),
        V((GR, RC, 128), F32),
        V((2, C, BC, 128), F32),
        V((2, C, GR, BC, 128), F32),
        V((C, BC, 128), F32),
        V((X * GR, C, BC, 128), F32),
        V((2, HB, D), F32),
        V((2, HB, D), BF16),
        V((2, HB, D), BF16),
        V((TC, D), F32),
        V((Z, OB, D), BF16),
        V((Z - 1, OB, D), BF16),
        V((2, Y, HB // Y, D), BF16),
        V((2, Y - 1, HB // Y, D), BF16),
        V((2, Y, HB // Y, D), BF16),
        S((3,)),
        S, S,
        S, S((X,)),
        S, S((X,)),
        S((3,)), S((3,)),
        S, S,
        S, S,
        S((5,)), S((6,)),
        S, S((X,)),
        S((2,)), S((2,)),
        S, S,
        S((2,)), S((2,)),
        S((2,)), S((2,)),
    ]
    return kernel, scratch


def place(gz_ref, gc_ref, gz_out, gc_out, sem):
    copies = [
        pltpu.make_async_copy(gz_ref, gz_out, sem.at[0]),
        pltpu.make_async_copy(gc_ref, gc_out, sem.at[1]),
    ]
    for copy in copies:
        copy.start()
    for copy in copies:
        copy.wait()


def body(embeddings, prototypes, pair_index):
    B, D = embeddings.shape
    NCL = prototypes.shape[0]
    NC = NCL // C
    OB = NCL // (X * Z * C)
    kernel, scratch = make_kernel(B, D, NC)
    vm = pl.BlockSpec(memory_space=pltpu.VMEM)
    hbm = pl.BlockSpec(memory_space=pl.ANY)
    shapes = (jax.ShapeDtypeStruct((B, D), F32), jax.ShapeDtypeStruct((OB, D), F32))
    held = (pltpu.VMEM((B, D), F32), pltpu.VMEM((OB, D), F32))
    grads = pl.pallas_call(
        kernel,
        out_shape=held,
        in_specs=[hbm, hbm, hbm],
        out_specs=(vm, vm),
        scratch_shapes=scratch,
        compiler_params=pltpu.CompilerParams(
            collective_id=0, has_side_effects=True, vmem_limit_bytes=60 * 2**20
        ),
        name="swav",
    )(embeddings, prototypes.reshape(X * Z, C, OB, D), pair_index.reshape(1, B))
    return pl.pallas_call(
        place,
        out_shape=shapes,
        in_specs=[vm, vm],
        out_specs=(hbm, hbm),
        scratch_shapes=[pltpu.SemaphoreType.DMA((2,))],
        name="place",
    )(*(pltpu.with_memory_space_constraint(g, pltpu.VMEM) for g in grads))


def solution(mesh):
    return jax.shard_map(
        body,
        mesh=mesh,
        in_specs=(P("dp", None), P("proto", None), P("dp")),
        out_specs=(P("dp", None), P(("proto", "dp"), None)),
        check_vma=False,
    )
```

time: 64.4 us -> 59.7 us (0.927)
  Pallas kernels: 63.7 us -> 58.8 us
    pallas_call x2, Pallas kernels: 63.7 us -> 58.8 us  [the longest x1 58 us: body(): pl.pallas_call(kernel, out_shape=held, in_specs=[hbm, hbm, hbm], out_spec...]
where the time goes in v3:
time: 59.7 us; the launch traced here: 59.6 us
  Pallas kernels  58.8 us (98%)
  between operations  0.8 us (1%)
    pallas_call x1, Pallas kernels, body(): pl.pallas_call(kernel, out_shape=held, in_specs=[hbm, hbm, hbm], out_spec...  58 us

profile of v3, /device:TPU:1, one launch (start us, length us, event | category | flops | bytes accessed | tf_op | source)
XLA Modules:
  0.0 59.6 jit_solution(6046908416956024541)
XLA Ops:
  0.6 58.0 %swav.1 = (f32[512,256]{1,0:T(8,128)S(1)}, f32[64,256]{1,0:T(8,128)S(1)}) custom-call(bf16[512,256]{1,0:T(8,128)(2,1)} %emb_ref.1, bf16[32,2,64,256]{3,2,1,0:T(8,128)(2,1)} %bitcast.2, s32[1,512]{1,0:T(1,128)} %bitcast.3), custom_call_target="tpu_custom_call" | custom-call | tf_op jit(solution)/shard_map/swav/pallas_call | solution.py:489
  58.6 0.8 %place.1 = (f32[512,256]{1,0:T(8,128)}, f32[64,256]{1,0:T(8,128)}) custom-call(f32[512,256]{1,0:T(8,128)S(1)} %get-tuple-element.4.gz_ref, f32[64,256]{1,0:T(8,128)S(1)} %get-tuple-element.5.gc_ref), custom_call_target="tpu_custom_call" | custom-call | tf_op jit(solution)/shard_map/place/pallas_call | solution.py:500

commit v4 on v3

--- a/solution.py
+++ b/solution.py
@@ -61,10 +61,10 @@
 
     def kernel(
         emb_ref, proto_ref, pair_ref, gz_ref, gc_ref,
-        pair_v, emb_v, zu, praw, chat, chato, ep, perm, permt, zall, E, K, ET, WT, colacc, racc, rb, rpb, c3a, c3b, mine_c,
+        pair_v, emb_v, zu, praw, chat, chato, ep, perm, permt, zall, K, KT, P1, precv, pown, TP, U, urecv, colacc, racc, rb, c3a, c3b, mine_c,
         crow, rrow, rp4, r34, csend, crecv, fsend, frecv, tsend, trecv, rsend, rrecv, rsend3, rrecv3,
-        gpart, ksend, krecv, tpart, zsend, zrecv, ysend, yrecv, yall,
-        lsem, core_s, core_r, xs, xr, fs, fr, cs, cr, f_s, f_r, ts, tr, rs, rr, ps, pr, ks, kr, zs, zr, ys, yr, gs, gr,
+        gpart, tpart, zsend, zrecv, ysend, yrecv, yall,
+        lsem, core_s, core_r, xs, xr, fs, fr, cs, cr, f_s, f_r, ts, tr, rs, rr, ps, pr, p_s, p_r, ks, kr, zs, zr, ys, yr, gs, gr,
     ):
         dp = lax.axis_index("dp")
         iy = lax.axis_index("proto")
@@ -89,7 +89,8 @@
         loads = [
             pltpu.make_async_copy(pair_ref, pair_v, lsem.at[0]),
             pltpu.make_async_copy(emb_ref, emb_v, lsem.at[1]),
-            pltpu.make_async_copy(proto_ref, praw, lsem.at[2]),
+            pltpu.make_async_copy(proto_ref.at[:, 1 - ic], praw.at[1], lsem.at[2]),
+            pltpu.make_async_copy(proto_ref.at[:, ic], praw.at[0], lsem.at[3]),
         ]
         for load in loads:
             load.start()
@@ -102,12 +103,11 @@
         loads[0].wait()
         v = emb_v[...].astype(F32)
         zu[...] = (v * (1.0 / jnp.sqrt(jnp.sum(v * v, axis=1, keepdims=True) + 1e-06))).astype(BF16)
-        loads[2].wait()
         NB = 256 // OB
 
         def norm_c(half, out):
             def step(i, _):
-                v = praw[pl.ds(i * NB, NB), half].reshape(256, D).astype(F32)
+                v = praw[half, pl.ds(i * NB, NB)].reshape(256, D).astype(F32)
                 inv = 1.0 / jnp.sqrt(jnp.sum(v * v, axis=1, keepdims=True) + 1e-06)
                 out[pl.ds(pl.multiple_of(i * 256, 256), 256), :] = (v * inv).astype(BF16)
                 return 0
@@ -122,9 +122,11 @@
             for j in range(CC):
                 out[j : j + 1, :] = jnp.sum(colacc[:, j * 128 : (j + 1) * 128], axis=0, keepdims=True)
 
-        norm_c(1 - ic, chato)
-        norm_c(ic, chat)
+        loads[2].wait()
+        norm_c(1, chato)
         first_totals(chato, fsend)
+        loads[3].wait()
+        norm_c(0, chat)
         pl.semaphore_wait(barrier, len(everyone))
         send(fsend, frecv, f_s, f_r, (0, 0, 1, 0))
         first_totals(chat, crow)
@@ -152,9 +154,9 @@
             for j in js:
                 cols = slice(j * 256, (j + 1) * 256)
                 e = jnp.exp(dot(zb, chat[cols, :], NT) * 10.0)
-                E[rows, cols] = e
-                k = e * e
-                K[rows, cols] = k
+                K[rows, cols] = e * e
+                part = dot(e.astype(BF16), chat[cols, :])
+                P1[h] = part if j == 0 else P1[h] + part
                 two = e[:, :128] + e[:, 128:]
                 racc[rows, :] = two if j == 0 else racc[rows, :] + two
 
@@ -171,15 +173,12 @@
             take(crecv.at[t], cr.at[t])
             crow[...] = 1.0 / jnp.sum(crecv[t].astype(F32), axis=0)
 
-        def row_pass(out, blocks, keep):
+        def row_pass(out, blocks):
             for i in range(blocks[0] * BC, (blocks[-1] + 1) * BC):
                 rows = slice(i * 128, (i + 1) * 128)
                 acc = jnp.zeros((128, 128), F32)
                 for j in range(CC):
-                    w = K[rows, j * 128 : (j + 1) * 128] * crow[j : j + 1, :]
-                    if keep:
-                        K[rows, j * 128 : (j + 1) * 128] = w
-                    acc = acc + w
+                    acc = acc + K[rows, j * 128 : (j + 1) * 128] * crow[j : j + 1, :]
                 out[i // BC, i % BC : i % BC + 1, :] = jnp.sum(acc.T, axis=0, keepdims=True)
 
         def col_pass(t):
@@ -203,7 +202,7 @@
 
         def row_send(t):
             for blk in range(C):
-                row_pass(rsend.at[t], (blk,), False)
+                row_pass(rsend.at[t], (blk,))
                 for i, o in enumerate(YC):
                     send(rsend.at[t, blk], rrecv.at[t, blk, i + 1], rs.at[t * C + blk], rr.at[t * C + blk], o)
                 pltpu.make_async_copy(rsend.at[t, blk], rrecv.at[t, blk, 0], rr.at[t * C + blk]).start()
@@ -212,14 +211,16 @@
             mine = mine_c[...]
             for c in range(C):
                 for q in range(B // 256):
-                    n = (a * C + c) * (B // 256) + q
-                    e = jnp.exp(dot(mine, zall[a, c, q * 256 : (q + 1) * 256, :], NT) * 10.0)
-                    for half in range(2):
-                        cols = slice(n * 256 + half * 128, n * 256 + (half + 1) * 128)
-                        i = c * BC + q * 2 + half
-                        eh = e[:, half * 128 : (half + 1) * 128]
-                        WT[:, cols] = eh * eh
-                        ET[:, cols] = eh * rp4[a, i : i + 1, :]
+                    n = (a * C + c) * (B // 256)
+                    zb = zall[a, c, q * 256 : (q + 1) * 256, :]
+                    e = jnp.exp(dot(mine, zb, NT) * 10.0)
+                    KT[:, (n + 1 - q) * 256 : (n + 2 - q) * 256] = (e * e).astype(BF16)
+                    i = c * BC + q * 2
+                    p = [
+                        (e[:, h * 128 : (h + 1) * 128] * rp4[a, i + h : i + h + 1, :]).astype(BF16) for h in range(2)
+                    ]
+                    part = dot(jnp.concatenate(p, axis=1), zb)
+                    TP[...] = part if a + c + q == 0 else TP[...] + part
 
         def send_x(a):
             send(zall.at[0, ic], zall.at[a, ic], xs, xr.at[a], (a, 0, 0, 0))
@@ -241,6 +242,7 @@
         scores(ic, range(NC // 256))
         take(zall.at[0, 1 - ic], core_r)
         scores(1 - ic, range(NC // 256))
+        send(P1.at[1 - ic], precv, p_s, p_r, (0, 0, 1, 0))
         for i in range(RC):
             tsend[i : i + 1, :] = jnp.sum(racc[i * 128 : (i + 1) * 128, :].T, axis=0, keepdims=True)
         for i, o in enumerate(YC):
@@ -255,30 +257,22 @@
         rp4[0] = 10.0 / jnp.sum(trecv[...], axis=0)
         for a in range(1, X):
             send(rp4.at[0], rp4.at[a], ps, pr.at[a], (a, 0, 0, 0))
+
+        col_pass(0)
+        col_send(1)
+        take(precv, p_r)
+        for i in range(BC):
+            rows = slice(i * 128, (i + 1) * 128)
+            rp = spread(rp4[0, pl.ds(ic * BC + i, 1), :])
+            pown[rows, :] = (P1[ic, rows, :] + precv[rows, :]) * jnp.concatenate([rp, rp], axis=1)
+        scores_t(0)
         for half, a in enumerate(NEAR):
             take(zall.at[a, ic], xr.at[a])
             relay(a, half)
         for a in NEAR:
             forward(a)
-
-        col_pass(0)
-        col_send(1)
-        for i in range(RC):
-            rpb[i * 128 : (i + 1) * 128, :] = spread(rp4[0, i : i + 1, :])
-
-        def scale(i, _):
-            rows = pl.ds(pl.multiple_of(i * 64, 64), 64)
-            rp = rpb[rows, :]
-            for j in range(CC):
-                E[rows, j * 128 : (j + 1) * 128] = E[rows, j * 128 : (j + 1) * 128] * rp
-            return 0
-
-        lax.fori_loop(0, RT // 64, scale, 0)
-        scores_t(0)
         col_take(1)
         row_send(1)
-        take(zall.at[FAR, ic], xr.at[FAR])
-        forward(FAR)
         for a in NEAR:
             take(rp4.at[a], pr.at[a])
             take(zall.at[a, 1 - ic], fr.at[a])
@@ -286,54 +280,48 @@
 
         col_pass(1)
         col_send(2)
+        take(zall.at[FAR, ic], xr.at[FAR])
+        forward(FAR)
         take(rp4.at[FAR], pr.at[FAR])
         take(zall.at[FAR, 1 - ic], fr.at[FAR])
         scores_t(FAR)
         col_take(2)
-        row_pass(rsend3, range(C), True)
+        row_pass(rsend3, range(C))
         for o in sorted(XYC, key=lambda o: o[0] != 0):
             send(rsend3, rrecv3.at[o[0] * GR + YCI[(0,) + o[1:]]], rs.at[4], rr.at[5 if o[0] else 4], o)
         pltpu.make_async_copy(rsend3, rrecv3.at[0], rr.at[4]).start()
+        def codes(h):
+            for q in range(2):
+                rows = pl.ds(pl.multiple_of(h * B + q * HB, HB), HB)
+                w = [(K[rows, j * 128 : (j + 1) * 128] * crow[j : j + 1, :]).astype(BF16) for j in range(CC)]
+                U[h, q] = dot(jnp.concatenate(w, axis=1), chat[...])
+
+        codes(1 - ic)
+        send(U.at[1 - ic], urecv, ks, kr, (0, 0, 1, 0))
+        codes(ic)
         mine = crow[pl.ds(ix * (TC // 128), TC // 128), :]
         for i in range(TC // 128):
             c3a[i * 128 : (i + 1) * 128, :] = spread(mine[i : i + 1, :])
         for k, b in enumerate(FZ):
             c3b[k * OB : (k + 1) * OB, :] = c3a[pl.ds(pl.multiple_of((iz + b) % Z * OB, OB), OB), :]
-        c3 = c3b[...]
-        for n in range(X * RC):
-            cols = slice(n * 128, (n + 1) * 128)
-            WT[:, cols] = WT[:, cols] * c3
+        take(urecv, kr)
+        U[ic] = U[ic] + urecv[...]
         take(rrecv3.at[pl.ds(0, GR)], rr.at[4])
         r34[0] = 10.0 / jnp.sum(rrecv3[0:GR], axis=0).reshape(RC, 128)
-        for i in range(RC):
-            rb[i * 128 : (i + 1) * 128, :] = spread(r34[0, i : i + 1, :])
-
-        def grad_r(h, out):
-            for q in range(2):
-                rows = pl.ds(pl.multiple_of(h * B + q * HB, HB), HB)
-                prows = pl.ds(pl.multiple_of(h * B + (1 - q) * HB, HB), HB)
-                r3 = rb[prows, :]
-                g = [
-                    (E[rows, j * 128 : (j + 1) * 128] - K[prows, j * 128 : (j + 1) * 128] * r3).astype(BF16)
-                    for j in range(CC)
-                ]
-                out[q] = dot(jnp.concatenate(g, axis=1), chat[...]).astype(out.dtype)
-
-        grad_r(1 - ic, ksend)
+        for i in range(BC):
+            q, rows = i * 128 // HB, slice(i * 128 % HB, i * 128 % HB + 128)
+            r3 = spread(r34[0, pl.ds(ic * BC + i, 1), :])
+            mine = pown[(1 - q) * HB + i * 128 % HB : (1 - q) * HB + i * 128 % HB + 128, :]
+            gpart[1 - q, rows, :] = mine - U[ic, q, rows, :] * jnp.concatenate([r3, r3], axis=1)
+        far_y = sorted(range(1, Y), key=lambda k: -ring(k, Y))
         for q in range(2):
-            send(ksend.at[q], krecv.at[q], ks.at[q], kr.at[q], (0, 0, 1, 0))
-        grad_r(ic, gpart)
+            ysend[q] = gpart[q].reshape(Y, HB // Y, D).astype(BF16)
+            for f in far_y:
+                send(ysend.at[q, (iy + f) % Y], yrecv.at[q, f - 1], ys.at[q], yr.at[q], (0, 0, 0, f))
+
         take(rrecv3.at[pl.ds(GR, (X - 1) * GR)], rr.at[5])
         for a in range(1, X):
             r34[a] = 10.0 / jnp.sum(rrecv3[a * GR : (a + 1) * GR], axis=0).reshape(RC, 128)
-        far_y = sorted(range(1, Y), key=lambda k: -ring(k, Y))
-        for q in range(2):
-            take(krecv.at[q], kr.at[q])
-            gpart[q] = gpart[q] + krecv[q].astype(F32)
-            ysend[q] = gpart[q].reshape(Y, HB // Y, D).astype(BF16)
-            for f in far_y:
-                send(ysend.at[q, (iy + f) % Y], yrecv.at[q, f - 1], ys.at[q], yr.at[q], (0, 0, 0, f))
-
         HT, ZH = TC // 2, Z // 2
 
         def grad_t(m, _):
@@ -342,9 +330,10 @@
             for n in range(X * RC):
                 a, q = n // RC, n % RC
                 qp = q // BC * BC + (q + BC // 2) % BC
-                cols, pcols = slice(n * 128, (n + 1) * 128), slice((a * RC + qp) * 128, (a * RC + qp + 1) * 128)
-                g.append((ET[rows, cols] - WT[rows, pcols] * r34[a, qp : qp + 1, :]).astype(BF16))
+                g.append(KT[rows, n * 128 : (n + 1) * 128] * r34[a, qp : qp + 1, :].astype(BF16))
             part = dot(jnp.concatenate(g, axis=1), zall[...].reshape(X * RT, D))
+            c3 = c3b[rows, :]
+            part = TP[rows, :] - part * jnp.concatenate([c3, c3], axis=1)
             tpart[rows, :] = part
             zsend[pl.ds(m * ZH, ZH)] = part.reshape(ZH, OB, D).astype(BF16)
             for k in range(ZH):
@@ -377,7 +366,7 @@
 
         take(zrecv, zr)
         gcs = tpart[(Z - 1) * OB : Z * OB, :] + jnp.sum(zrecv[...].astype(F32), axis=0)
-        uc, nc = unit(praw[ix * Z + iz, ic].astype(F32))
+        uc, nc = unit(praw[0, ix * Z + iz].astype(F32))
         gc_ref[...] = (gcs - uc * jnp.sum(uc * gcs, axis=1, keepdims=True)) / nc
         for q in range(2):
             take(yall.at[q, pl.ds(0, Y - 1)], gr.at[q])
@@ -390,6 +379,8 @@
         for t in range(3):
             take(crecv.at[t, pl.ds(0, len(XZ))], cs.at[t])
         take(fsend, f_s)
+        take(precv, p_s)
+        take(urecv, ks)
         take(trecv.at[pl.ds(0, len(YC))], ts)
         for t in range(2):
             for blk in range(C):
@@ -397,7 +388,6 @@
         take(rrecv3.at[pl.ds(0, len(XYC))], rs.at[4])
         take(zrecv, zs)
         for q in range(2):
-            take(ksend.at[q], ks.at[q])
             take(yrecv.at[q], ys.at[q])
             take(yall.at[q, pl.ds(0, Y - 1)], gs.at[q])
 
@@ -407,7 +397,7 @@
         V((1, B), jnp.int32),
         V((B, D), BF16),
         V((B, D), BF16),
-        V((X * Z, C, OB, D), BF16),
+        V((C, X * Z, OB, D), BF16),
         V((NC, D), BF16),
         V((NC, D), BF16),
         V((B, D), BF16),
@@ -415,13 +405,16 @@
         V((B, B), BF16),
         V((X, C, B, D), BF16),
         V((RT, NC), F32),
-        V((RT, NC), F32),
-        V((TC, X * RT), F32),
-        V((TC, X * RT), F32),
+        V((TC, X * RT), BF16),
+        V((C, B, D), F32),
+        V((B, D), F32),
+        V((B, D), F32),
+        V((TC, D), F32),
+        V((C, 2, HB, D), F32),
+        V((2, HB, D), F32),
         V((8, NC), F32),
         V((RT, 128), F32),
-        V((RT, 128), F32),
-        V((RT, 128), F32),
+        V((B, 128), F32),
         V((TC, 128), F32),
         V((TC, 128), F32),
         V((TC, D), BF16),
@@ -440,15 +433,13 @@
         V((C, BC, 128), F32),
         V((X * GR, C, BC, 128), F32),
         V((2, HB, D), F32),
-        V((2, HB, D), BF16),
-        V((2, HB, D), BF16),
         V((TC, D), F32),
         V((Z, OB, D), BF16),
         V((Z - 1, OB, D), BF16),
         V((2, Y, HB // Y, D), BF16),
         V((2, Y - 1, HB // Y, D), BF16),
         V((2, Y, HB // Y, D), BF16),
-        S((3,)),
+        S((4,)),
         S, S,
         S, S((X,)),
         S, S((X,)),
@@ -457,7 +448,8 @@
         S, S,
         S((5,)), S((6,)),
         S, S((X,)),
-        S((2,)), S((2,)),
+        S, S,
+        S, S,
         S, S,
         S((2,)), S((2,)),
         S((2,)), S((2,)),

time: 59.7 us -> 57.8 us (0.968)
  Pallas kernels: 58.8 us -> 56.9 us
    pallas_call x1, Pallas kernels: 58 us -> 56.1 us  [body(): pl.pallas_call(kernel, out_shape=held, in_specs=[hbm, hbm, hbm], out_spec...]
where the time goes in v4:
time: 57.8 us; the launch traced here: 57.7 us
  Pallas kernels  56.9 us (98%)
  between operations  0.8 us (1%)
    pallas_call x1, Pallas kernels, body(): pl.pallas_call(kernel, out_shape=held, in_specs=[hbm, hbm, hbm], out_spec...  56.1 us

profile of v4, /device:TPU:1, one launch (start us, length us, event | category | flops | bytes accessed | tf_op | source)
XLA Modules:
  0.0 57.7 jit_solution(4995822127380658924)
XLA Ops:
  0.6 56.1 %swav.1 = (f32[512,256]{1,0:T(8,128)S(1)}, f32[64,256]{1,0:T(8,128)S(1)}) custom-call(bf16[512,256]{1,0:T(8,128)(2,1)} %emb_ref.1, bf16[32,2,64,256]{3,2,1,0:T(8,128)(2,1)} %bitcast.2, s32[1,512]{1,0:T(1,128)} %bitcast.3), custom_call_target="tpu_custom_call" | custom-call | tf_op jit(solution)/shard_map/swav/pallas_call | solution.py:481
  56.7 0.8 %place.1 = (f32[512,256]{1,0:T(8,128)}, f32[64,256]{1,0:T(8,128)}) custom-call(f32[512,256]{1,0:T(8,128)S(1)} %get-tuple-element.4.gz_ref, f32[64,256]{1,0:T(8,128)S(1)} %get-tuple-element.5.gc_ref), custom_call_target="tpu_custom_call" | custom-call | tf_op jit(solution)/shard_map/place/pallas_call | solution.py:492

commit v5 on v4

--- a/solution.py
+++ b/solution.py
@@ -319,6 +319,16 @@
             for f in far_y:
                 send(ysend.at[q, (iy + f) % Y], yrecv.at[q, f - 1], ys.at[q], yr.at[q], (0, 0, 0, f))
 
+        def codes_t(rows, sources):
+            g = []
+            for n in range(sources[0] * RC, (sources[-1] + 1) * RC):
+                a, q = n // RC, n % RC
+                qp = q // BC * BC + (q + BC // 2) % BC
+                g.append(KT[rows, n * 128 : (n + 1) * 128] * r34[a, qp : qp + 1, :].astype(BF16))
+            zb = zall[sources[0] : sources[-1] + 1].reshape(len(sources) * RT, D)
+            return dot(jnp.concatenate(g, axis=1), zb)
+
+        tpart[...] = codes_t(slice(0, TC), (0,))
         take(rrecv3.at[pl.ds(GR, (X - 1) * GR)], rr.at[5])
         for a in range(1, X):
             r34[a] = 10.0 / jnp.sum(rrecv3[a * GR : (a + 1) * GR], axis=0).reshape(RC, 128)
@@ -326,12 +336,7 @@
 
         def grad_t(m, _):
             rows = pl.ds(pl.multiple_of(m * HT, HT), HT)
-            g = []
-            for n in range(X * RC):
-                a, q = n // RC, n % RC
-                qp = q // BC * BC + (q + BC // 2) % BC
-                g.append(KT[rows, n * 128 : (n + 1) * 128] * r34[a, qp : qp + 1, :].astype(BF16))
-            part = dot(jnp.concatenate(g, axis=1), zall[...].reshape(X * RT, D))
+            part = tpart[rows, :] + codes_t(rows, range(1, X))
             c3 = c3b[rows, :]
             part = TP[rows, :] - part * jnp.concatenate([c3, c3], axis=1)
             tpart[rows, :] = part
@@ -355,22 +360,23 @@
         lax.fori_loop(0, 2, grad_t, 0)
 
         SB = HB // Y
+        uc, nc = unit(praw[0, ix * Z + iz].astype(F32))
+        units = [unit(ep[pl.ds(pl.multiple_of(q * HB + iy * SB, SB), SB), :].astype(F32)) for q in range(2)]
         for q in range(2):
+            uq, nq = units[q]
             take(yrecv.at[q], yr.at[q])
             at = pl.ds(pl.multiple_of(iy * SB, SB), SB)
             gzs = gpart[q, at, :] + jnp.sum(yrecv[q].astype(F32), axis=0)
-            uq, nq = unit(ep[pl.ds(pl.multiple_of(q * HB + iy * SB, SB), SB), :].astype(F32))
             yall[q, iy] = ((gzs - uq * jnp.sum(uq * gzs, axis=1, keepdims=True)) / nq).astype(BF16)
             for f in far_y:
                 send(yall.at[q, iy], yall.at[q, iy], gs.at[q], gr.at[q], (0, 0, 0, f))
 
-        take(zrecv, zr)
-        gcs = tpart[(Z - 1) * OB : Z * OB, :] + jnp.sum(zrecv[...].astype(F32), axis=0)
-        uc, nc = unit(praw[0, ix * Z + iz].astype(F32))
-        gc_ref[...] = (gcs - uc * jnp.sum(uc * gcs, axis=1, keepdims=True)) / nc
         for q in range(2):
             take(yall.at[q, pl.ds(0, Y - 1)], gr.at[q])
         gz_ref[...] = dot(permt[...], yall[...].reshape(B, D))
+        take(zrecv, zr)
+        gcs = tpart[(Z - 1) * OB : Z * OB, :] + jnp.sum(zrecv[...].astype(F32), axis=0)
+        gc_ref[...] = (gcs - uc * jnp.sum(uc * gcs, axis=1, keepdims=True)) / nc
 
         take(zall.at[0, ic], core_s)
         take(zall.at[pl.ds(0, X - 1), 0], xs)
@@ -458,10 +464,11 @@
 
 
 def place(gz_ref, gc_ref, gz_out, gc_out, sem):
-    copies = [
-        pltpu.make_async_copy(gz_ref, gz_out, sem.at[0]),
-        pltpu.make_async_copy(gc_ref, gc_out, sem.at[1]),
-    ]
+    step = gz_ref.shape[0] // 4
+    copies = [pltpu.make_async_copy(gc_ref, gc_out, sem.at[4])]
+    for i in range(4):
+        rows = pl.ds(i * step, step)
+        copies.append(pltpu.make_async_copy(gz_ref.at[rows], gz_out.at[rows], sem.at[i]))
     for copy in copies:
         copy.start()
     for copy in copies:
@@ -494,7 +501,7 @@
         out_shape=shapes,
         in_specs=[vm, vm],
         out_specs=(hbm, hbm),
-        scratch_shapes=[pltpu.SemaphoreType.DMA((2,))],
+        scratch_shapes=[pltpu.SemaphoreType.DMA((5,))],
         name="place",
     )(*(pltpu.with_memory_space_constraint(g, pltpu.VMEM) for g in grads))
 

time: 57.8 us -> 57.3 us (level)
  no operation moved by 1% of the time
where the time goes in v5:
time: 57.3 us; the launch traced here: 57.2 us
  Pallas kernels  56.4 us (98%)
  between operations  0.8 us (1%)
    pallas_call x1, Pallas kernels, body(): pl.pallas_call(kernel, out_shape=held, in_specs=[hbm, hbm, hbm], out_spec...  55.6 us

profile of v5, /device:TPU:1, one launch (start us, length us, event | category | flops | bytes accessed | tf_op | source)
XLA Modules:
  0.0 57.2 jit_solution(11008318488807552537)
XLA Ops:
  0.6 55.6 %swav.1 = (f32[512,256]{1,0:T(8,128)S(1)}, f32[64,256]{1,0:T(8,128)S(1)}) custom-call(bf16[512,256]{1,0:T(8,128)(2,1)} %emb_ref.1, bf16[32,2,64,256]{3,2,1,0:T(8,128)(2,1)} %bitcast.2, s32[1,512]{1,0:T(1,128)} %bitcast.3), custom_call_target="tpu_custom_call" | custom-call | tf_op jit(solution)/shard_map/swav/pallas_call | solution.py:488
  56.2 0.9 %place.1 = (f32[512,256]{1,0:T(8,128)}, f32[64,256]{1,0:T(8,128)}) custom-call(f32[512,256]{1,0:T(8,128)S(1)} %get-tuple-element.4.gz_ref, f32[64,256]{1,0:T(8,128)S(1)} %get-tuple-element.5.gc_ref), custom_call_target="tpu_custom_call" | custom-call | tf_op jit(solution)/shard_map/place/pallas_call | solution.py:499

commit v6 on v5

--- a/solution.py
+++ b/solution.py
@@ -332,7 +332,8 @@
         take(rrecv3.at[pl.ds(GR, (X - 1) * GR)], rr.at[5])
         for a in range(1, X):
             r34[a] = 10.0 / jnp.sum(rrecv3[a * GR : (a + 1) * GR], axis=0).reshape(RC, 128)
-        HT, ZH = TC // 2, Z // 2
+        parts = 4
+        HT, ZH = TC // parts, Z // parts
 
         def grad_t(m, _):
             rows = pl.ds(pl.multiple_of(m * HT, HT), HT)
@@ -354,10 +355,10 @@
                 if k < ZH - 1:
                     go()
                 else:
-                    pl.when(m == 0)(go)
+                    pl.when(m < parts - 1)(go)
             return 0
 
-        lax.fori_loop(0, 2, grad_t, 0)
+        lax.fori_loop(0, parts, grad_t, 0)
 
         SB = HB // Y
         uc, nc = unit(praw[0, ix * Z + iz].astype(F32))

time: 57.3 us -> 57.1 us (level)
  no operation moved by 1% of the time
where the time goes in v6:
time: 57.1 us; the launch traced here: 57 us
  Pallas kernels  56.2 us (98%)
  between operations  0.8 us (1%)
    pallas_call x1, Pallas kernels, body(): pl.pallas_call(kernel, out_shape=held, in_specs=[hbm, hbm, hbm], out_spec...  55.3 us

profile of v6, /device:TPU:1, one launch (start us, length us, event | category | flops | bytes accessed | tf_op | source)
XLA Modules:
  0.0 57.0 jit_solution(11581739321313734373)
XLA Ops:
  0.6 55.3 %swav.1 = (f32[512,256]{1,0:T(8,128)S(1)}, f32[64,256]{1,0:T(8,128)S(1)}) custom-call(bf16[512,256]{1,0:T(8,128)(2,1)} %emb_ref.1, bf16[32,2,64,256]{3,2,1,0:T(8,128)(2,1)} %bitcast.2, s32[1,512]{1,0:T(1,128)} %bitcast.3), custom_call_target="tpu_custom_call" | custom-call | tf_op jit(solution)/shard_map/swav/pallas_call | solution.py:489
  56.0 0.9 %place.1 = (f32[512,256]{1,0:T(8,128)}, f32[64,256]{1,0:T(8,128)}) custom-call(f32[512,256]{1,0:T(8,128)S(1)} %get-tuple-element.4.gz_ref, f32[64,256]{1,0:T(8,128)S(1)} %get-tuple-element.5.gc_ref), custom_call_target="tpu_custom_call" | custom-call | tf_op jit(solution)/shard_map/place/pallas_call | solution.py:500

commit v7 on v6

--- a/solution.py
+++ b/solution.py
@@ -290,22 +290,24 @@
         for o in sorted(XYC, key=lambda o: o[0] != 0):
             send(rsend3, rrecv3.at[o[0] * GR + YCI[(0,) + o[1:]]], rs.at[4], rr.at[5 if o[0] else 4], o)
         pltpu.make_async_copy(rsend3, rrecv3.at[0], rr.at[4]).start()
-        def codes(h):
+        def codes(h, other):
             for q in range(2):
                 rows = pl.ds(pl.multiple_of(h * B + q * HB, HB), HB)
                 w = [(K[rows, j * 128 : (j + 1) * 128] * crow[j : j + 1, :]).astype(BF16) for j in range(CC)]
                 U[h, q] = dot(jnp.concatenate(w, axis=1), chat[...])
-
-        codes(1 - ic)
-        send(U.at[1 - ic], urecv, ks, kr, (0, 0, 1, 0))
-        codes(ic)
+                if other:
+                    send(U.at[h, q], urecv.at[q], ks.at[q], kr.at[q], (0, 0, 1, 0))
+
+        codes(1 - ic, True)
+        codes(ic, False)
         mine = crow[pl.ds(ix * (TC // 128), TC // 128), :]
         for i in range(TC // 128):
             c3a[i * 128 : (i + 1) * 128, :] = spread(mine[i : i + 1, :])
         for k, b in enumerate(FZ):
             c3b[k * OB : (k + 1) * OB, :] = c3a[pl.ds(pl.multiple_of((iz + b) % Z * OB, OB), OB), :]
-        take(urecv, kr)
-        U[ic] = U[ic] + urecv[...]
+        for q in range(2):
+            take(urecv.at[q], kr.at[q])
+            U[ic, q] = U[ic, q] + urecv[q]
         take(rrecv3.at[pl.ds(0, GR)], rr.at[4])
         r34[0] = 10.0 / jnp.sum(rrecv3[0:GR], axis=0).reshape(RC, 128)
         for i in range(BC):
@@ -387,7 +389,8 @@
             take(crecv.at[t, pl.ds(0, len(XZ))], cs.at[t])
         take(fsend, f_s)
         take(precv, p_s)
-        take(urecv, ks)
+        for q in range(2):
+            take(urecv.at[q], ks.at[q])
         take(trecv.at[pl.ds(0, len(YC))], ts)
         for t in range(2):
             for blk in range(C):
@@ -456,7 +459,7 @@
         S((5,)), S((6,)),
         S, S((X,)),
         S, S,
-        S, S,
+        S((2,)), S((2,)),
         S, S,
         S((2,)), S((2,)),
         S((2,)), S((2,)),

time: 57.1 us -> 57.1 us (level)
  no operation moved by 1% of the time
where the time goes in v7:
time: 57.1 us; the launch traced here: 57 us
  Pallas kernels  56.2 us (98%)
  between operations  0.8 us (1%)
    pallas_call x1, Pallas kernels, body(): pl.pallas_call(kernel, out_shape=held, in_specs=[hbm, hbm, hbm], out_spec...  55.4 us

profile of v7, /device:TPU:1, one launch (start us, length us, event | category | flops | bytes accessed | tf_op | source)
XLA Modules:
  0.0 57.0 jit_solution(2378544192564509515)
XLA Ops:
  0.6 55.4 %swav.1 = (f32[512,256]{1,0:T(8,128)S(1)}, f32[64,256]{1,0:T(8,128)S(1)}) custom-call(bf16[512,256]{1,0:T(8,128)(2,1)} %emb_ref.1, bf16[32,2,64,256]{3,2,1,0:T(8,128)(2,1)} %bitcast.2, s32[1,512]{1,0:T(1,128)} %bitcast.3), custom_call_target="tpu_custom_call" | custom-call | tf_op jit(solution)/shard_map/swav/pallas_call | solution.py:492
  56.0 0.9 %place.1 = (f32[512,256]{1,0:T(8,128)}, f32[64,256]{1,0:T(8,128)}) custom-call(f32[512,256]{1,0:T(8,128)S(1)} %get-tuple-element.4.gz_ref, f32[64,256]{1,0:T(8,128)S(1)} %get-tuple-element.5.gc_ref), custom_call_target="tpu_custom_call" | custom-call | tf_op jit(solution)/shard_map/place/pallas_call | solution.py:503
